TPU v7x, 32 devices: a whole 2x2x4 slice. The times are simulated.
32 devices in a mesh: pipe: 2 (over core), rows: 16 (over z, y, x).
Axes of the slice: x: 2, y: 2, z: 4, core: 2. Of those that a mesh axis runs over, the one named last changes fastest.
Arguments:
- section_in: bfloat16 [2, 4, 64, 24, 2048], P('pipe', None, 'rows'), may hold values from -12 to 12
- image_start: int32 [4, 64], replicated, may hold values from 0 to 1, as said below
- pool_choice: int32 [4, 32, 12], P(None, 'rows'), may hold values from 0 to 3
- conv_shared: bfloat16 [2, 2, 4608, 512], P('pipe'), may hold values from -0.09375 to 0.09375
- task_in: bfloat16 [2, 3, 1024, 512], P('pipe'), may hold values from -0.1875 to 0.1875
- task_mid: bfloat16 [2, 3, 512, 512], P('pipe'), may hold values from -0.25 to 0.25
- task_conv: bfloat16 [2, 3, 4608, 512], P('pipe'), may hold values from -0.09375 to 0.09375
- bn_gain: float32 [2, 11, 512], P('pipe'), may hold values from 0.25 to 1.75
- bn_bias: float32 [2, 11, 512], P('pipe'), may hold values from -2 to 2
Outputs:
- section_out: bfloat16 [2, 4, 64, 24, 2048], P('pipe', None, 'rows')
- conv_shared_grad: float32 [2, 2, 2359296], P('pipe', None, 'rows')
- task_in_grad: float32 [2, 3, 524288], P('pipe', None, 'rows')
- task_mid_grad: float32 [2, 3, 262144], P('pipe', None, 'rows')
- task_conv_grad: float32 [2, 3, 2359296], P('pipe', None, 'rows')
- bn_gain_grad: float32 [2, 11, 512], P('pipe')
- bn_bias_grad: float32 [2, 11, 512], P('pipe')
Inputs may be any that keep to these rules, and one draw needn't show every extreme that they name: `image_start`: in each micro-batch, 1 on every 18-th row, from an even first row below 18 drawn from the seed; in one micro-batch, drawn from the seed, every row is 0.
All inputs are finite; a program needn't handle non-finite values.
Results may differ from a plain program's by a relative error of at most 0.023.
Values may be sent and summed in bfloat16 or wider, within the bound.
A program may use at most 320 MiB of HBM per device.

v0:
```python
import jax
import jax.numpy as jnp
from jax import lax
from jax.sharding import PartitionSpec as P

epsilon = 1e-05
half_type = jnp.bfloat16


def padded_2(block, sides, width):
    for axis, dim in sides:
        count = lax.axis_size(axis)
        forward = [(i, i + 1) for i in range(count - 1)]
        backward = [(target, source) for source, target in forward]
        low = lax.ppermute(
            lax.slice_in_dim(block, block.shape[dim] - width, None, axis=dim), axis, forward
        )
        high = lax.ppermute(lax.slice_in_dim(block, 0, width, axis=dim), axis, backward)
        block = jnp.concatenate([low, block, high], axis=dim)
    return block


def for_sending(shard):
    return jax.tree.map(lambda a: a.astype(jnp.bfloat16) if a.dtype == jnp.float32 else a, shard)


def passed_along(shard, axis, by):
    size = lax.axis_size(axis)
    pairs = [(i, i + by) for i in range(size) if 0 <= i + by < size]
    return lax.ppermute(shard, axis, pairs)


def band_masks(start_table, batch_number, height):
    whole_row = lax.dynamic_index_in_dim(start_table, batch_number, 0, keepdims=False)
    extended = jnp.concatenate([whole_row, jnp.zeros((1,), jnp.int32)])
    first_row = lax.axis_index("rows") * height
    window = lax.dynamic_slice_in_dim(extended, first_row, height + 1, 0).astype(jnp.float32)
    upper_ok = 1.0 - window[:height]
    lower_ok = 1.0 - window[1:]
    return (upper_ok.astype(half_type), lower_ok.astype(half_type))


def forward_taps(padded, upper_ok, lower_ok):
    height = padded.shape[0] - 2
    columns = padded.shape[1]
    above_rows = padded[:height] * upper_ok[:, None, None]
    below_rows = padded[2:] * lower_ok[:, None, None]
    pieces = []
    for shifted in (above_rows, padded[1 : height + 1], below_rows):
        widened = jnp.pad(shifted, ((0, 0), (1, 1), (0, 0)))
        for offset in range(3):
            pieces.append(widened[:, offset : offset + columns])
    return jnp.concatenate(pieces, -1)


def backward_taps(padded, upper_ok, lower_ok):
    height = padded.shape[0] - 2
    columns = padded.shape[1]
    from_below = padded[2:] * lower_ok[:, None, None]
    from_above = padded[:height] * upper_ok[:, None, None]
    pieces = []
    for shifted in (from_below, padded[1 : height + 1], from_above):
        widened = jnp.pad(shifted, ((0, 0), (1, 1), (0, 0)))
        for offset in range(3):
            pieces.append(widened[:, 2 - offset : 2 - offset + columns])
    return jnp.stack(pieces, 2)


def conv_forward(feature, kernel, upper_ok, lower_ok):
    padded = padded_2(feature, (("rows", 0),), 1)
    stacked = forward_taps(padded, upper_ok, lower_ok)
    return (padded, jnp.einsum("rwk,ko->rwo", stacked, kernel, preferred_element_type=jnp.float32))


def conv_backward(gradient, padded_input, kernel, upper_ok, lower_ok):
    padded = padded_2(for_sending(gradient), (("rows", 0),), 1).astype(gradient.dtype)
    stacked = backward_taps(padded, upper_ok, lower_ok)
    channels = gradient.shape[2]
    kernel_blocks = kernel.reshape(9, channels, channels)
    grad_into = jnp.einsum(
        "rwbo,bco->rwc", stacked, kernel_blocks, preferred_element_type=jnp.float32
    )
    kernel_grad = jnp.einsum(
        "rwk,rwo->ko",
        forward_taps(padded_input, upper_ok, lower_ok),
        gradient,
        preferred_element_type=jnp.float32,
    )
    return (grad_into, kernel_grad)


def batch_moments(tensors, pixels):
    totals = tuple((jnp.sum(member, (0, 1)) for member in tensors)) + tuple(
        (jnp.sum(member * member, (0, 1)) for member in tensors)
    )
    totals = lax.psum(totals, "rows")
    how_many = len(tensors)
    results = []
    for number in range(how_many):
        average = totals[number] / pixels
        spread = totals[how_many + number] / pixels - average * average
        results.append((average, lax.rsqrt(spread + epsilon)))
    return results


def norm_back(entries, pixels):
    totals = tuple((jnp.sum(entry[0], (0, 1)) for entry in entries)) + tuple(
        (jnp.sum(entry[0] * entry[1], (0, 1)) for entry in entries)
    )
    totals = lax.psum(totals, "rows")
    how_many = len(entries)
    results = []
    for number in range(how_many):
        grad_norm, normed, gain_row, scale_row = entries[number]
        shift_sum = totals[number]
        scale_sum = totals[how_many + number]
        grad_pre = (
            gain_row * scale_row * (grad_norm - shift_sum / pixels - normed * scale_sum / pixels)
        )
        results.append((grad_pre.astype(half_type), shift_sum, scale_sum))
    return results


def apply_norm(tensor, stats, gain_row, bias_row):
    return (tensor - stats[0]) * stats[1] * gain_row + bias_row


def local_grad(function, point, upstream):
    outcome, pullback = jax.vjp(function, point)
    return pullback(upstream)[0]


def pack_terms(members, bands):
    parts = []
    for member in members:
        count = member.shape[0]
        parts.append(member.reshape(count, bands, -1).transpose(1, 0, 2).reshape(bands, -1))
    return jnp.concatenate(parts, 1)


def unpack_terms(flat, layout):
    results = []
    offset = 0
    for count, share in layout:
        results.append(flat[offset : offset + count * share].reshape(count, share))
        offset = offset + count * share
    return tuple(results)


def section_forward(shared, branches, upper_ok, lower_ok, params, pixels):
    conv_kernels, joint_kernels, middle_kernels, branch_kernels, gain_rows, biases = params
    channels = shared.shape[2]
    tasks = joint_kernels.shape[0]
    padded_shared, pre_one = conv_forward(shared, conv_kernels[0], upper_ok, lower_ok)
    (stats_one,) = batch_moments((pre_one,), pixels)
    hidden_one = jax.nn.silu(apply_norm(pre_one, stats_one, gain_rows[0], biases[0])).astype(
        half_type
    )
    padded_hidden, pre_two = conv_forward(hidden_one, conv_kernels[1], upper_ok, lower_ok)
    pre_three = []
    for task in range(tasks):
        joined = jnp.concatenate(
            [hidden_one, branches[..., task * channels : (task + 1) * channels]], -1
        )
        pre_three.append(
            jnp.einsum(
                "rwc,co->rwo", joined, joint_kernels[task], preferred_element_type=jnp.float32
            )
        )
    found = batch_moments((pre_two,) + tuple(pre_three), pixels)
    stats_two = found[0]
    hidden_two = jax.nn.silu(apply_norm(pre_two, stats_two, gain_rows[1], biases[1])).astype(
        half_type
    )
    pre_four = []
    for task in range(tasks):
        base = 2 + 3 * task
        branch_act = jax.nn.silu(
            apply_norm(pre_three[task], found[1 + task], gain_rows[base], biases[base])
        ).astype(half_type)
        pre_four.append(
            jnp.einsum(
                "rwc,co->rwo", branch_act, middle_kernels[task], preferred_element_type=jnp.float32
            )
        )
    stats_four = batch_moments(tuple(pre_four), pixels)
    padded_products = []
    pre_five = []
    for task in range(tasks):
        base = 2 + 3 * task
        gating = jax.nn.sigmoid(
            apply_norm(pre_four[task], stats_four[task], gain_rows[base + 1], biases[base + 1])
        )
        product = (gating * hidden_two).astype(half_type)
        padded_product, pre_result = conv_forward(product, branch_kernels[task], upper_ok, lower_ok)
        padded_products.append(padded_product)
        pre_five.append(pre_result)
    stats_five = batch_moments(tuple(pre_five), pixels)
    results = [hidden_two]
    outputs = [pre_one, pre_two]
    all_stats = [stats_one, stats_two]
    for task in range(tasks):
        base = 2 + 3 * task
        results.append(
            jax.nn.silu(
                apply_norm(pre_five[task], stats_five[task], gain_rows[base + 2], biases[base + 2])
            ).astype(half_type)
        )
        outputs.extend([pre_three[task], pre_four[task], pre_five[task]])
        all_stats.extend([found[1 + task], stats_four[task], stats_five[task]])
    kept_state = (
        padded_shared,
        padded_hidden,
        tuple(padded_products),
        branches,
        tuple(outputs),
        tuple(all_stats),
    )
    return (jnp.concatenate(results, -1), kept_state)


def section_backward(grad_hidden, grad_branches, kept_state, upper_ok, lower_ok, params, pixels):
    conv_kernels, joint_kernels, middle_kernels, branch_kernels, gain_rows, biases = params
    padded_shared, padded_hidden, padded_products, branches, outputs, stats = kept_state
    tasks = joint_kernels.shape[0]
    count = len(outputs)
    normed = [(outputs[number] - stats[number][0]) * stats[number][1] for number in range(count)]
    shifted = [normed[number] * gain_rows[number] + biases[number] for number in range(count)]
    hidden_one = padded_hidden[1:-1]
    channels = hidden_one.shape[2]
    hidden_two = jax.nn.silu(shifted[1]).astype(half_type)
    per_norm = [None] * count
    fifth_entries = []
    for task in range(tasks):
        base = 2 + 3 * task
        grad_five = local_grad(
            jax.nn.silu,
            shifted[base + 2],
            grad_branches[..., task * channels : (task + 1) * channels],
        )
        fifth_entries.append((grad_five, normed[base + 2], gain_rows[base + 2], stats[base + 2][1]))
    fifth = norm_back(tuple(fifth_entries), pixels)
    grad_two = grad_hidden
    fourth_entries = []
    kernel_fives = []
    for task in range(tasks):
        base = 2 + 3 * task
        per_norm[base + 2] = fifth[task]
        gating = jax.nn.sigmoid(shifted[base + 1])
        grad_product, kernel_five = conv_backward(
            fifth[task][0], padded_products[task], branch_kernels[task], upper_ok, lower_ok
        )
        kernel_fives.append(kernel_five)
        grad_two = grad_two + grad_product * gating
        pre_grad_four = local_grad(jax.nn.sigmoid, shifted[base + 1], grad_product * hidden_two)
        fourth_entries.append(
            (pre_grad_four, normed[base + 1], gain_rows[base + 1], stats[base + 1][1])
        )
    pre_grad_two = local_grad(jax.nn.silu, shifted[1], grad_two)
    second = norm_back(
        ((pre_grad_two, normed[1], gain_rows[1], stats[1][1]),) + tuple(fourth_entries), pixels
    )
    per_norm[1] = second[0]
    grad_from_conv, kernel_two = conv_backward(
        second[0][0], padded_hidden, conv_kernels[1], upper_ok, lower_ok
    )
    third_entries = []
    kernel_fours = []
    for task in range(tasks):
        base = 2 + 3 * task
        per_norm[base + 1] = second[1 + task]
        back_four = second[1 + task][0]
        branch_act = jax.nn.silu(shifted[base]).astype(half_type)
        grad_act = jnp.einsum(
            "rwo,co->rwc", back_four, middle_kernels[task], preferred_element_type=jnp.float32
        )
        kernel_fours.append(
            jnp.einsum("rwc,rwo->co", branch_act, back_four, preferred_element_type=jnp.float32)
        )
        pre_grad_three = local_grad(jax.nn.silu, shifted[base], grad_act)
        third_entries.append((pre_grad_three, normed[base], gain_rows[base], stats[base][1]))
    third = norm_back(tuple(third_entries), pixels)
    grad_one = grad_from_conv
    branch_grads = []
    kernel_threes = []
    for task in range(tasks):
        base = 2 + 3 * task
        per_norm[base] = third[task]
        back_three = third[task][0]
        joined = jnp.concatenate(
            [hidden_one, branches[..., task * channels : (task + 1) * channels]], -1
        )
        grad_joined = jnp.einsum(
            "rwo,co->rwc", back_three, joint_kernels[task], preferred_element_type=jnp.float32
        )
        kernel_threes.append(
            jnp.einsum("rwc,rwo->co", joined, back_three, preferred_element_type=jnp.float32)
        )
        grad_one = grad_one + grad_joined[..., :channels]
        branch_grads.append(grad_joined[..., channels:])
    pre_grad_one = local_grad(jax.nn.silu, shifted[0], grad_one)
    (first,) = norm_back(((pre_grad_one, normed[0], gain_rows[0], stats[0][1]),), pixels)
    per_norm[0] = first
    grad_shared, kernel_one = conv_backward(
        first[0], padded_shared, conv_kernels[0], upper_ok, lower_ok
    )
    kernels = (
        jnp.stack([kernel_one, kernel_two]),
        jnp.stack(kernel_threes),
        jnp.stack(kernel_fours),
        jnp.stack(kernel_fives),
    )
    gain_grad = jnp.stack([entry[2] for entry in per_norm])
    bias_grad = jnp.stack([entry[1] for entry in per_norm])
    return (jnp.concatenate([grad_shared] + branch_grads, -1), kernels, gain_grad, bias_grad)


def spread_grad(pooled):
    widened = jnp.repeat(jnp.repeat(pooled.astype(jnp.float32), 2, 0), 2, 1)
    return widened * 0.25


def window_pick(selector):
    height, across = selector.shape
    onehot = (selector[:, :, None] == jnp.arange(4, dtype=jnp.int32)).astype(half_type)
    return onehot.reshape(height, across, 2, 2).transpose(0, 2, 1, 3)


def unpool(pooled, picker):
    height, across, channels = pooled.shape
    return (pooled[:, None, :, None, :] * picker[..., None]).reshape(
        2 * height, 2 * across, channels
    )


def unpool_back(gradient, picker):
    height, across, channels = gradient.shape
    folded = gradient.reshape(height // 2, 2, across // 2, 2, channels) * picker[..., None]
    return jnp.sum(folded, (1, 3))


def pool_mean(tensor):
    height, across, channels = tensor.shape
    folded = tensor.astype(jnp.float32).reshape(height // 2, 2, across // 2, 2, channels)
    return jnp.mean(folded, (1, 3)).astype(half_type)


def per_device(
    section_in,
    image_start,
    pool_choice,
    conv_shared,
    task_in,
    task_mid,
    task_conv,
    bn_gain,
    bn_bias,
):
    leading = lax.axis_index("pipe") == 0
    section_data = section_in[0]
    batches, height, across, all_channels = section_data.shape
    channels = conv_shared.shape[3]
    tasks = task_in.shape[1]
    shared_count = conv_shared.shape[1]
    bands = lax.axis_size("rows")
    pixels = float(height * across * bands)
    params = (conv_shared[0], task_in[0], task_mid[0], task_conv[0], bn_gain[0], bn_bias[0])
    layout = (
        (shared_count, 9 * channels * channels // bands),
        (tasks, 2 * channels * channels // bands),
        (tasks, channels * channels // bands),
        (tasks, 9 * channels * channels // bands),
    )

    def forward_step(received, step_number):
        first_batch = jnp.minimum(step_number, batches - 1)
        second_batch = jnp.maximum(step_number - 1, 0)
        chosen = jnp.where(leading, first_batch, second_batch)
        upper_ok, lower_ok = band_masks(image_start, chosen, height)
        picker = window_pick(lax.dynamic_index_in_dim(pool_choice, second_batch, 0, keepdims=False))
        opened = unpool(received, picker)
        own_batch = lax.dynamic_index_in_dim(section_data, first_batch, 0, keepdims=False)
        source = jnp.where(leading, own_batch, opened)
        result_rows, kept_state = section_forward(
            source[..., :channels], source[..., channels:], upper_ok, lower_ok, params, pixels
        )
        passed_on = passed_along(pool_mean(result_rows), "pipe", 1)
        return (passed_on, (kept_state, upper_ok, lower_ok, picker, result_rows))

    start_pooled = jnp.zeros((height // 2, across // 2, all_channels), half_type)
    step_numbers = jnp.arange(batches + 1, dtype=jnp.int32)
    ignored, memory = lax.scan(forward_step, start_pooled, step_numbers)
    kept_all, uppers, lowers, pickers, result_all = memory
    start_sums = (
        jnp.zeros((shared_count, 9 * channels * channels), jnp.float32),
        jnp.zeros((tasks, 2 * channels * channels), jnp.float32),
        jnp.zeros((tasks, channels * channels), jnp.float32),
        jnp.zeros((tasks, 9 * channels * channels), jnp.float32),
    )

    def backward_step(state_now, slot_data):
        position, kept_state, upper_ok, lower_ok, picker = slot_data
        sent_back, gain_total, bias_total, sums_now = state_now
        step_number = batches - position
        cotangent_batch = jnp.maximum(batches - 1 - step_number, 0)
        cotangent = lax.dynamic_index_in_dim(
            section_data, cotangent_batch, 0, keepdims=False
        ).astype(jnp.float32)
        incoming = jnp.where(leading, spread_grad(sent_back), cotangent)
        joined_grad, kernels, gain_grad, bias_grad = section_backward(
            incoming[..., :channels],
            incoming[..., channels:],
            kept_state,
            upper_ok,
            lower_ok,
            params,
            pixels,
        )
        useful = jnp.where(leading, step_number >= 1, step_number < batches)
        flat_terms = tuple(
            (jnp.where(useful, member, 0.0).reshape(member.shape[0], -1) for member in kernels)
        )
        gain_total = gain_total + jnp.where(useful, gain_grad, 0.0)
        bias_total = bias_total + jnp.where(useful, bias_grad, 0.0)
        sums_now = tuple((total_part + member for total_part, member in zip(sums_now, flat_terms)))
        back_pooled = unpool_back(joined_grad, picker).astype(half_type)
        new_sent = passed_along(back_pooled, "pipe", -1)
        return ((new_sent, gain_total, bias_total, sums_now), joined_grad.astype(half_type))

    start_state = (
        start_pooled,
        jnp.zeros(bn_gain.shape[1:], jnp.float32),
        jnp.zeros(bn_bias.shape[1:], jnp.float32),
        start_sums,
    )
    final_state, grads_all = lax.scan(
        backward_step, start_state, (step_numbers, kept_all, uppers, lowers, pickers), reverse=True
    )
    unused_sent, gain_total, bias_total, summed = final_state
    packed = lax.psum_scatter(pack_terms(summed, bands), "rows", scatter_dimension=0, tiled=True)
    whole_shares = unpack_terms(packed[0], layout)
    decoded = result_all[1:]
    encoded = grads_all[:batches]
    result = jnp.where(leading, encoded, decoded)[None]
    return (
        result,
        whole_shares[0][None],
        whole_shares[1][None],
        whole_shares[2][None],
        whole_shares[3][None],
        gain_total[None],
        bias_total[None],
    )


def solution(mesh):
    in_specs = (
        P("pipe", None, "rows", None, None),
        P(),
        P(None, "rows", None),
        P("pipe", None, None, None),
        P("pipe", None, None, None),
        P("pipe", None, None, None),
        P("pipe", None, None, None),
        P("pipe", None, None),
        P("pipe", None, None),
    )
    out_specs = (
        P("pipe", None, "rows", None, None),
        P("pipe", None, "rows"),
        P("pipe", None, "rows"),
        P("pipe", None, "rows"),
        P("pipe", None, "rows"),
        P("pipe", None, None),
        P("pipe", None, None),
    )
    return jax.shard_map(
        per_device, mesh=mesh, in_specs=in_specs, out_specs=out_specs, check_vma=False
    )
```

profile of v0, /device:TPU:8, one launch (start us, length us, event | category | flops | bytes accessed | tf_op | source)
XLA Modules:
  0.0 6606.9 jit_solution(10806546188873560154)
XLA Ops:
  9.9 1813.1 %while.127 = (s32[]{:T(128)}, bf16[2,12,2048]{2,1,0:T(8,128)(2,1)S(1)}, bf16[5,6,24,512]{3,2,1,0:T(8,128)(2,1)}, bf16[5,6,24,512]{3,2,1,0:T(8,128)(2,1)}, bf16[5...) while((s32[]{:T(128)}, ...), condition=%wide.region_46.47_spmd, body=%wide.region_0.46_spmd.sunk | while | flops 2734600192 | bytes 63721632 | solution.py:392
  74.2 71.2 %all-reduce.63 = (f32[512]{0:T(512)S(1)}, f32[512]{0:T(512)S(1)}, f32[512]{0:T(512)S(1)}, f32[512]{0:T(512)S(1)}, f32[512]{0:T(512)S(1)}, /*index=5*/f32[512]{0:T(512)S(1)}) all-reduce(f32[512]{0:T(512)S(1)} %get-tuple-element.3593, f32[512]{0:T(512)S(1)} %get-tuple-element.3594, ...), channel_id=1, replica_groups=mesh['pipe'=2,'rows'=16] {'rows'}, use_global_device_ids=true, to_apply=%region_36.36 | all-reduce | flops 3072 | bytes 24576 | tf_op jit(solution)/shard_map/while/body/eval_jaxpr/psum | solution.py:96
  167.4 71.8 %all-reduce.64 = (f32[512]{0:T(512)S(1)}, f32[512]{0:T(512)S(1)}, f32[512]{0:T(512)S(1)}, f32[512]{0:T(512)S(1)}, f32[512]{0:T(512)S(1)}, /*index=5*/f32[512]{0:T(512)S(1)}, f32[512]{0:T(512)S(1)}, f32[512]{0:T(512)S(1)}) all-reduce(f32[512]{0:T(512)S(1)} %get-tuple-element.3611, ...), channel_id=1, replica_groups=mesh['pipe'=2,'rows'=16] {'rows'}, use_global_device_ids=true, to_apply=%region_8.8 | all-reduce | flops 4096 | bytes 32768 | tf_op jit(solution)/shard_map/while/body/eval_jaxpr/psum | solution.py:96
  283.6 69.6 %all-reduce.65 = (f32[512]{0:T(512)S(1)}, f32[512]{0:T(512)S(1)}, f32[512]{0:T(512)S(1)}, f32[512]{0:T(512)S(1)}, f32[512]{0:T(512)S(1)}, /*index=5*/f32[512]{0:T(512)S(1)}) all-reduce(f32[512]{0:T(512)S(1)} %get-tuple-element.3676, f32[512]{0:T(512)S(1)} %get-tuple-element.3677, ...), channel_id=1, replica_groups=mesh['pipe'=2,'rows'=16] {'rows'}, use_global_device_ids=true, to_apply=%region_44.44 | all-reduce | flops 3072 | bytes 24576 | tf_op jit(solution)/shard_map/while/body/eval_jaxpr/psum | solution.py:96
  387.2 36.2 all-reduce.62
  438.3 70.9 %all-reduce.63 = (f32[512]{0:T(512)S(1)}, f32[512]{0:T(512)S(1)}, f32[512]{0:T(512)S(1)}, f32[512]{0:T(512)S(1)}, f32[512]{0:T(512)S(1)}, /*index=5*/f32[512]{0:T(512)S(1)}) all-reduce(f32[512]{0:T(512)S(1)} %get-tuple-element.3593, f32[512]{0:T(512)S(1)} %get-tuple-element.3594, ...), channel_id=1, replica_groups=mesh['pipe'=2,'rows'=16] {'rows'}, use_global_device_ids=true, to_apply=%region_36.36 | all-reduce | flops 3072 | bytes 24576 | tf_op jit(solution)/shard_map/while/body/eval_jaxpr/psum | solution.py:96
  531.2 71.8 %all-reduce.64 = (f32[512]{0:T(512)S(1)}, f32[512]{0:T(512)S(1)}, f32[512]{0:T(512)S(1)}, f32[512]{0:T(512)S(1)}, f32[512]{0:T(512)S(1)}, /*index=5*/f32[512]{0:T(512)S(1)}, f32[512]{0:T(512)S(1)}, f32[512]{0:T(512)S(1)}) all-reduce(f32[512]{0:T(512)S(1)} %get-tuple-element.3611, ...), channel_id=1, replica_groups=mesh['pipe'=2,'rows'=16] {'rows'}, use_global_device_ids=true, to_apply=%region_8.8 | all-reduce | flops 4096 | bytes 32768 | tf_op jit(solution)/shard_map/while/body/eval_jaxpr/psum | solution.py:96
  647.4 69.6 %all-reduce.65 = (f32[512]{0:T(512)S(1)}, f32[512]{0:T(512)S(1)}, f32[512]{0:T(512)S(1)}, f32[512]{0:T(512)S(1)}, f32[512]{0:T(512)S(1)}, /*index=5*/f32[512]{0:T(512)S(1)}) all-reduce(f32[512]{0:T(512)S(1)} %get-tuple-element.3676, f32[512]{0:T(512)S(1)} %get-tuple-element.3677, ...), channel_id=1, replica_groups=mesh['pipe'=2,'rows'=16] {'rows'}, use_global_device_ids=true, to_apply=%region_44.44 | all-reduce | flops 3072 | bytes 24576 | tf_op jit(solution)/shard_map/while/body/eval_jaxpr/psum | solution.py:96
  751.0 36.1 all-reduce.62
  802.0 70.9 %all-reduce.63 = (f32[512]{0:T(512)S(1)}, f32[512]{0:T(512)S(1)}, f32[512]{0:T(512)S(1)}, f32[512]{0:T(512)S(1)}, f32[512]{0:T(512)S(1)}, /*index=5*/f32[512]{0:T(512)S(1)}) all-reduce(f32[512]{0:T(512)S(1)} %get-tuple-element.3593, f32[512]{0:T(512)S(1)} %get-tuple-element.3594, ...), channel_id=1, replica_groups=mesh['pipe'=2,'rows'=16] {'rows'}, use_global_device_ids=true, to_apply=%region_36.36 | all-reduce | flops 3072 | bytes 24576 | tf_op jit(solution)/shard_map/while/body/eval_jaxpr/psum | solution.py:96
  895.0 71.8 %all-reduce.64 = (f32[512]{0:T(512)S(1)}, f32[512]{0:T(512)S(1)}, f32[512]{0:T(512)S(1)}, f32[512]{0:T(512)S(1)}, f32[512]{0:T(512)S(1)}, /*index=5*/f32[512]{0:T(512)S(1)}, f32[512]{0:T(512)S(1)}, f32[512]{0:T(512)S(1)}) all-reduce(f32[512]{0:T(512)S(1)} %get-tuple-element.3611, ...), channel_id=1, replica_groups=mesh['pipe'=2,'rows'=16] {'rows'}, use_global_device_ids=true, to_apply=%region_8.8 | all-reduce | flops 4096 | bytes 32768 | tf_op jit(solution)/shard_map/while/body/eval_jaxpr/psum | solution.py:96
  1011.1 69.6 %all-reduce.65 = (f32[512]{0:T(512)S(1)}, f32[512]{0:T(512)S(1)}, f32[512]{0:T(512)S(1)}, f32[512]{0:T(512)S(1)}, f32[512]{0:T(512)S(1)}, /*index=5*/f32[512]{0:T(512)S(1)}) all-reduce(f32[512]{0:T(512)S(1)} %get-tuple-element.3676, f32[512]{0:T(512)S(1)} %get-tuple-element.3677, ...), channel_id=1, replica_groups=mesh['pipe'=2,'rows'=16] {'rows'}, use_global_device_ids=true, to_apply=%region_44.44 | all-reduce | flops 3072 | bytes 24576 | tf_op jit(solution)/shard_map/while/body/eval_jaxpr/psum | solution.py:96
  1114.8 36.2 all-reduce.62
  1165.8 70.9 %all-reduce.63 = (f32[512]{0:T(512)S(1)}, f32[512]{0:T(512)S(1)}, f32[512]{0:T(512)S(1)}, f32[512]{0:T(512)S(1)}, f32[512]{0:T(512)S(1)}, /*index=5*/f32[512]{0:T(512)S(1)}) all-reduce(f32[512]{0:T(512)S(1)} %get-tuple-element.3593, f32[512]{0:T(512)S(1)} %get-tuple-element.3594, ...), channel_id=1, replica_groups=mesh['pipe'=2,'rows'=16] {'rows'}, use_global_device_ids=true, to_apply=%region_36.36 | all-reduce | flops 3072 | bytes 24576 | tf_op jit(solution)/shard_map/while/body/eval_jaxpr/psum | solution.py:96
  1258.8 71.8 %all-reduce.64 = (f32[512]{0:T(512)S(1)}, f32[512]{0:T(512)S(1)}, f32[512]{0:T(512)S(1)}, f32[512]{0:T(512)S(1)}, f32[512]{0:T(512)S(1)}, /*index=5*/f32[512]{0:T(512)S(1)}, f32[512]{0:T(512)S(1)}, f32[512]{0:T(512)S(1)}) all-reduce(f32[512]{0:T(512)S(1)} %get-tuple-element.3611, ...), channel_id=1, replica_groups=mesh['pipe'=2,'rows'=16] {'rows'}, use_global_device_ids=true, to_apply=%region_8.8 | all-reduce | flops 4096 | bytes 32768 | tf_op jit(solution)/shard_map/while/body/eval_jaxpr/psum | solution.py:96
  1374.9 69.6 %all-reduce.65 = (f32[512]{0:T(512)S(1)}, f32[512]{0:T(512)S(1)}, f32[512]{0:T(512)S(1)}, f32[512]{0:T(512)S(1)}, f32[512]{0:T(512)S(1)}, /*index=5*/f32[512]{0:T(512)S(1)}) all-reduce(f32[512]{0:T(512)S(1)} %get-tuple-element.3676, f32[512]{0:T(512)S(1)} %get-tuple-element.3677, ...), channel_id=1, replica_groups=mesh['pipe'=2,'rows'=16] {'rows'}, use_global_device_ids=true, to_apply=%region_44.44 | all-reduce | flops 3072 | bytes 24576 | tf_op jit(solution)/shard_map/while/body/eval_jaxpr/psum | solution.py:96
  1478.6 36.2 all-reduce.62
  1529.6 70.9 %all-reduce.63 = (f32[512]{0:T(512)S(1)}, f32[512]{0:T(512)S(1)}, f32[512]{0:T(512)S(1)}, f32[512]{0:T(512)S(1)}, f32[512]{0:T(512)S(1)}, /*index=5*/f32[512]{0:T(512)S(1)}) all-reduce(f32[512]{0:T(512)S(1)} %get-tuple-element.3593, f32[512]{0:T(512)S(1)} %get-tuple-element.3594, ...), channel_id=1, replica_groups=mesh['pipe'=2,'rows'=16] {'rows'}, use_global_device_ids=true, to_apply=%region_36.36 | all-reduce | flops 3072 | bytes 24576 | tf_op jit(solution)/shard_map/while/body/eval_jaxpr/psum | solution.py:96
  1622.5 71.8 %all-reduce.64 = (f32[512]{0:T(512)S(1)}, f32[512]{0:T(512)S(1)}, f32[512]{0:T(512)S(1)}, f32[512]{0:T(512)S(1)}, f32[512]{0:T(512)S(1)}, /*index=5*/f32[512]{0:T(512)S(1)}, f32[512]{0:T(512)S(1)}, f32[512]{0:T(512)S(1)}) all-reduce(f32[512]{0:T(512)S(1)} %get-tuple-element.3611, ...), channel_id=1, replica_groups=mesh['pipe'=2,'rows'=16] {'rows'}, use_global_device_ids=true, to_apply=%region_8.8 | all-reduce | flops 4096 | bytes 32768 | tf_op jit(solution)/shard_map/while/body/eval_jaxpr/psum | solution.py:96
  1738.7 69.6 %all-reduce.65 = (f32[512]{0:T(512)S(1)}, f32[512]{0:T(512)S(1)}, f32[512]{0:T(512)S(1)}, f32[512]{0:T(512)S(1)}, f32[512]{0:T(512)S(1)}, /*index=5*/f32[512]{0:T(512)S(1)}) all-reduce(f32[512]{0:T(512)S(1)} %get-tuple-element.3676, f32[512]{0:T(512)S(1)} %get-tuple-element.3677, ...), channel_id=1, replica_groups=mesh['pipe'=2,'rows'=16] {'rows'}, use_global_device_ids=true, to_apply=%region_44.44 | all-reduce | flops 3072 | bytes 24576 | tf_op jit(solution)/shard_map/while/body/eval_jaxpr/psum | solution.py:96
  1824.6 3198.8 %while.128 = (s32[]{:T(128)}, bf16[2,12,2048]{2,1,0:T(8,128)(2,1)S(1)}, f32[11,512]{1,0:T(8,128)}, f32[11,512]{1,0:T(8,128)}, f32[2,2359296]{1,0:T(2,128)}, /*in...) while((s32[]{:T(128)}, ...), condition=%wide.region_93.94_spmd.clone, body=%wide.region_47.93_spmd.clone.sunk | while | flops 5524090880 | bytes 658182848 | solution.py:436
  1836.4 71.8 %all-reduce.66 = (f32[512]{0:T(512)S(1)}, f32[512]{0:T(512)S(1)}, f32[512]{0:T(512)S(1)}, f32[512]{0:T(512)S(1)}, f32[512]{0:T(512)S(1)}, /*index=5*/f32[512]{0:T(512)S(1)}) all-reduce(f32[512]{0:T(512)S(1)} %get-tuple-element.3785, f32[512]{0:T(512)S(1)} %get-tuple-element.3786, ...), channel_id=1, replica_groups=mesh['pipe'=2,'rows'=16] {'rows'}, use_global_device_ids=true, to_apply=%region_59.59 | all-reduce | flops 3072 | bytes 24576 | tf_op jit(solution)/shard_map/while/body/eval_jaxpr/psum | solution.py:110
  2001.1 69.4 %all-reduce.67 = (f32[512]{0:T(512)S(1)}, f32[512]{0:T(512)S(1)}, f32[512]{0:T(512)S(1)}, f32[512]{0:T(512)S(1)}, f32[512]{0:T(512)}, /*index=5*/f32[512]{0:T(512)}) all-reduce(f32[512]{0:T(512)S(1)} %get-tuple-element.3814, f32[512]{0:T(512)S(1)} %get-tuple-element.3815, ...), channel_id=1, replica_groups=mesh['pipe'=2,'rows'=16] {'rows'}, use_global_device_ids=true, to_apply=%region_83.83 | all-reduce | flops 3072 | bytes 24576 | tf_op jit(solution)/shard_map/while/body/eval_jaxpr/psum | solution.py:110
  2092.2 71.7 %all-reduce.68 = (f32[512]{0:T(512)S(1)}, f32[512]{0:T(512)}, f32[512]{0:T(512)S(1)}, f32[512]{0:T(512)}, f32[512]{0:T(512)}, /*index=5*/f32[512]{0:T(512)}, f32[512]{0:T(512)}, f32[512]{0:T(512)}) all-reduce(f32[512]{0:T(512)} %get-tuple-element.3828, f32[512]{0:T(512)} %get-tuple-element.3829, ...), channel_id=1, replica_groups=mesh['pipe'=2,'rows'=16] {'rows'}, use_global_device_ids=true, to_apply=%region_87.87 | all-reduce | flops 4096 | bytes 32768 | tf_op jit(solution)/shard_map/while/body/eval_jaxpr/psum | solution.py:110
  2288.3 35.8 fusion.603
  2329.6 34.5 all-reduce.69
  2475.7 69.6 %all-reduce.66 = (f32[512]{0:T(512)S(1)}, f32[512]{0:T(512)S(1)}, f32[512]{0:T(512)S(1)}, f32[512]{0:T(512)S(1)}, f32[512]{0:T(512)S(1)}, /*index=5*/f32[512]{0:T(512)S(1)}) all-reduce(f32[512]{0:T(512)S(1)} %get-tuple-element.3785, f32[512]{0:T(512)S(1)} %get-tuple-element.3786, ...), channel_id=1, replica_groups=mesh['pipe'=2,'rows'=16] {'rows'}, use_global_device_ids=true, to_apply=%region_59.59 | all-reduce | flops 3072 | bytes 24576 | tf_op jit(solution)/shard_map/while/body/eval_jaxpr/psum | solution.py:110
  2638.1 69.4 %all-reduce.67 = (f32[512]{0:T(512)S(1)}, f32[512]{0:T(512)S(1)}, f32[512]{0:T(512)S(1)}, f32[512]{0:T(512)S(1)}, f32[512]{0:T(512)}, /*index=5*/f32[512]{0:T(512)}) all-reduce(f32[512]{0:T(512)S(1)} %get-tuple-element.3814, f32[512]{0:T(512)S(1)} %get-tuple-element.3815, ...), channel_id=1, replica_groups=mesh['pipe'=2,'rows'=16] {'rows'}, use_global_device_ids=true, to_apply=%region_83.83 | all-reduce | flops 3072 | bytes 24576 | tf_op jit(solution)/shard_map/while/body/eval_jaxpr/psum | solution.py:110
  2729.2 71.7 %all-reduce.68 = (f32[512]{0:T(512)S(1)}, f32[512]{0:T(512)}, f32[512]{0:T(512)S(1)}, f32[512]{0:T(512)}, f32[512]{0:T(512)}, /*index=5*/f32[512]{0:T(512)}, f32[512]{0:T(512)}, f32[512]{0:T(512)}) all-reduce(f32[512]{0:T(512)} %get-tuple-element.3828, f32[512]{0:T(512)} %get-tuple-element.3829, ...), channel_id=1, replica_groups=mesh['pipe'=2,'rows'=16] {'rows'}, use_global_device_ids=true, to_apply=%region_87.87 | all-reduce | flops 4096 | bytes 32768 | tf_op jit(solution)/shard_map/while/body/eval_jaxpr/psum | solution.py:110
  2925.3 36.5 fusion.603
  2967.3 34.5 all-reduce.69
  3113.8 69.6 %all-reduce.66 = (f32[512]{0:T(512)S(1)}, f32[512]{0:T(512)S(1)}, f32[512]{0:T(512)S(1)}, f32[512]{0:T(512)S(1)}, f32[512]{0:T(512)S(1)}, /*index=5*/f32[512]{0:T(512)S(1)}) all-reduce(f32[512]{0:T(512)S(1)} %get-tuple-element.3785, f32[512]{0:T(512)S(1)} %get-tuple-element.3786, ...), channel_id=1, replica_groups=mesh['pipe'=2,'rows'=16] {'rows'}, use_global_device_ids=true, to_apply=%region_59.59 | all-reduce | flops 3072 | bytes 24576 | tf_op jit(solution)/shard_map/while/body/eval_jaxpr/psum | solution.py:110
  3276.2 69.4 %all-reduce.67 = (f32[512]{0:T(512)S(1)}, f32[512]{0:T(512)S(1)}, f32[512]{0:T(512)S(1)}, f32[512]{0:T(512)S(1)}, f32[512]{0:T(512)}, /*index=5*/f32[512]{0:T(512)}) all-reduce(f32[512]{0:T(512)S(1)} %get-tuple-element.3814, f32[512]{0:T(512)S(1)} %get-tuple-element.3815, ...), channel_id=1, replica_groups=mesh['pipe'=2,'rows'=16] {'rows'}, use_global_device_ids=true, to_apply=%region_83.83 | all-reduce | flops 3072 | bytes 24576 | tf_op jit(solution)/shard_map/while/body/eval_jaxpr/psum | solution.py:110
  3367.3 71.7 %all-reduce.68 = (f32[512]{0:T(512)S(1)}, f32[512]{0:T(512)}, f32[512]{0:T(512)S(1)}, f32[512]{0:T(512)}, f32[512]{0:T(512)}, /*index=5*/f32[512]{0:T(512)}, f32[512]{0:T(512)}, f32[512]{0:T(512)}) all-reduce(f32[512]{0:T(512)} %get-tuple-element.3828, f32[512]{0:T(512)} %get-tuple-element.3829, ...), channel_id=1, replica_groups=mesh['pipe'=2,'rows'=16] {'rows'}, use_global_device_ids=true, to_apply=%region_87.87 | all-reduce | flops 4096 | bytes 32768 | tf_op jit(solution)/shard_map/while/body/eval_jaxpr/psum | solution.py:110
  3563.3 36.5 fusion.603
  3605.3 34.5 all-reduce.69
  3751.8 69.6 %all-reduce.66 = (f32[512]{0:T(512)S(1)}, f32[512]{0:T(512)S(1)}, f32[512]{0:T(512)S(1)}, f32[512]{0:T(512)S(1)}, f32[512]{0:T(512)S(1)}, /*index=5*/f32[512]{0:T(512)S(1)}) all-reduce(f32[512]{0:T(512)S(1)} %get-tuple-element.3785, f32[512]{0:T(512)S(1)} %get-tuple-element.3786, ...), channel_id=1, replica_groups=mesh['pipe'=2,'rows'=16] {'rows'}, use_global_device_ids=true, to_apply=%region_59.59 | all-reduce | flops 3072 | bytes 24576 | tf_op jit(solution)/shard_map/while/body/eval_jaxpr/psum | solution.py:110
  3914.2 69.4 %all-reduce.67 = (f32[512]{0:T(512)S(1)}, f32[512]{0:T(512)S(1)}, f32[512]{0:T(512)S(1)}, f32[512]{0:T(512)S(1)}, f32[512]{0:T(512)}, /*index=5*/f32[512]{0:T(512)}) all-reduce(f32[512]{0:T(512)S(1)} %get-tuple-element.3814, f32[512]{0:T(512)S(1)} %get-tuple-element.3815, ...), channel_id=1, replica_groups=mesh['pipe'=2,'rows'=16] {'rows'}, use_global_device_ids=true, to_apply=%region_83.83 | all-reduce | flops 3072 | bytes 24576 | tf_op jit(solution)/shard_map/while/body/eval_jaxpr/psum | solution.py:110
  4005.3 71.7 %all-reduce.68 = (f32[512]{0:T(512)S(1)}, f32[512]{0:T(512)}, f32[512]{0:T(512)S(1)}, f32[512]{0:T(512)}, f32[512]{0:T(512)}, /*index=5*/f32[512]{0:T(512)}, f32[512]{0:T(512)}, f32[512]{0:T(512)}) all-reduce(f32[512]{0:T(512)} %get-tuple-element.3828, f32[512]{0:T(512)} %get-tuple-element.3829, ...), channel_id=1, replica_groups=mesh['pipe'=2,'rows'=16] {'rows'}, use_global_device_ids=true, to_apply=%region_87.87 | all-reduce | flops 4096 | bytes 32768 | tf_op jit(solution)/shard_map/while/body/eval_jaxpr/psum | solution.py:110
  4201.4 36.5 fusion.603
  4243.4 34.5 all-reduce.69
  4389.9 69.6 %all-reduce.66 = (f32[512]{0:T(512)S(1)}, f32[512]{0:T(512)S(1)}, f32[512]{0:T(512)S(1)}, f32[512]{0:T(512)S(1)}, f32[512]{0:T(512)S(1)}, /*index=5*/f32[512]{0:T(512)S(1)}) all-reduce(f32[512]{0:T(512)S(1)} %get-tuple-element.3785, f32[512]{0:T(512)S(1)} %get-tuple-element.3786, ...), channel_id=1, replica_groups=mesh['pipe'=2,'rows'=16] {'rows'}, use_global_device_ids=true, to_apply=%region_59.59 | all-reduce | flops 3072 | bytes 24576 | tf_op jit(solution)/shard_map/while/body/eval_jaxpr/psum | solution.py:110
  4552.3 69.4 %all-reduce.67 = (f32[512]{0:T(512)S(1)}, f32[512]{0:T(512)S(1)}, f32[512]{0:T(512)S(1)}, f32[512]{0:T(512)S(1)}, f32[512]{0:T(512)}, /*index=5*/f32[512]{0:T(512)}) all-reduce(f32[512]{0:T(512)S(1)} %get-tuple-element.3814, f32[512]{0:T(512)S(1)} %get-tuple-element.3815, ...), channel_id=1, replica_groups=mesh['pipe'=2,'rows'=16] {'rows'}, use_global_device_ids=true, to_apply=%region_83.83 | all-reduce | flops 3072 | bytes 24576 | tf_op jit(solution)/shard_map/while/body/eval_jaxpr/psum | solution.py:110
  4643.4 71.7 %all-reduce.68 = (f32[512]{0:T(512)S(1)}, f32[512]{0:T(512)}, f32[512]{0:T(512)S(1)}, f32[512]{0:T(512)}, f32[512]{0:T(512)}, /*index=5*/f32[512]{0:T(512)}, f32[512]{0:T(512)}, f32[512]{0:T(512)}) all-reduce(f32[512]{0:T(512)} %get-tuple-element.3828, f32[512]{0:T(512)} %get-tuple-element.3829, ...), channel_id=1, replica_groups=mesh['pipe'=2,'rows'=16] {'rows'}, use_global_device_ids=true, to_apply=%region_87.87 | all-reduce | flops 4096 | bytes 32768 | tf_op jit(solution)/shard_map/while/body/eval_jaxpr/psum | solution.py:110
  4839.4 36.5 fusion.603
  4881.4 34.5 all-reduce.69
  5074.2 52.1 pad_maximum_fusion.33
  5131.6 1435.3 %all-reduce.72.cloned.1.call-done = f32[16,884736]{1,0:T(8,128)} async-done(((f32[16,884736]{1,0:T(8,128)}), f32[16,884736]{1,0:T(8,128)}) %all-reduce.72.cloned.1.call-update) | async-done | bytes 56623120
  (3469 shorter events, 2452.4 us)
Async XLA Ops:
  7.2 6559.8 %all-reduce.72.cloned.1.call-start = ((), (), s32[]{:S(2)}) async-start(), calls=%async_computation | async-start | bytes 113246208
  67.1 96.9 %collective-permute-start.2 = (bf16[1,24,512]{2,1,0:T(8,128)(2,1)S(1)}, bf16[1,24,512]{2,1,0:T(8,128)(2,1)S(1)}, u32[]{:S(2)}, u32[]{:S(2)}) collective-permute-start(bf16[1,24,512]{2,1,0:T(8,128)(2,1)S(1)} %get-tuple-element.3607), channel_id=1, source_target_pairs={{1,0},{2,1},{3,2},{4,3},{5,4},{6,5},{7,6},{8,7},{9,8},{10,9},{11,1... | collective-permute-start | bytes 73736 | tf_op jit(solution)/shard_map/while/body/eval_jaxpr/ppermute | solution.py:18
  71.6 92.0 %collective-permute-start.3 = (bf16[1,24,512]{2,1,0:T(8,128)(2,1)S(1)}, bf16[1,24,512]{2,1,0:T(8,128)(2,1)S(1)}, u32[]{:S(2)}, u32[]{:S(2)}) collective-permute-start(bf16[1,24,512]{2,1,0:T(8,128)(2,1)S(1)} %get-tuple-element.3608), channel_id=1, source_target_pairs={{0,1},{1,2},{2,3},{3,4},{4,5},{5,6},{6,7},{7,8},{8,9},{9,10},{10,1... | collective-permute-start | bytes 73736 | tf_op jit(solution)/shard_map/while/body/eval_jaxpr/ppermute | solution.py:15
  428.2 99.6 %collective-permute-start.2 = (bf16[1,24,512]{2,1,0:T(8,128)(2,1)S(1)}, bf16[1,24,512]{2,1,0:T(8,128)(2,1)S(1)}, u32[]{:S(2)}, u32[]{:S(2)}) collective-permute-start(bf16[1,24,512]{2,1,0:T(8,128)(2,1)S(1)} %get-tuple-element.3607), channel_id=1, source_target_pairs={{1,0},{2,1},{3,2},{4,3},{5,4},{6,5},{7,6},{8,7},{9,8},{10,9},{11,1... | collective-permute-start | bytes 73736 | tf_op jit(solution)/shard_map/while/body/eval_jaxpr/ppermute | solution.py:18
  435.6 91.7 %collective-permute-start.3 = (bf16[1,24,512]{2,1,0:T(8,128)(2,1)S(1)}, bf16[1,24,512]{2,1,0:T(8,128)(2,1)S(1)}, u32[]{:S(2)}, u32[]{:S(2)}) collective-permute-start(bf16[1,24,512]{2,1,0:T(8,128)(2,1)S(1)} %get-tuple-element.3608), channel_id=1, source_target_pairs={{0,1},{1,2},{2,3},{3,4},{4,5},{5,6},{6,7},{7,8},{8,9},{9,10},{10,1... | collective-permute-start | bytes 73736 | tf_op jit(solution)/shard_map/while/body/eval_jaxpr/ppermute | solution.py:15
  791.9 99.6 %collective-permute-start.2 = (bf16[1,24,512]{2,1,0:T(8,128)(2,1)S(1)}, bf16[1,24,512]{2,1,0:T(8,128)(2,1)S(1)}, u32[]{:S(2)}, u32[]{:S(2)}) collective-permute-start(bf16[1,24,512]{2,1,0:T(8,128)(2,1)S(1)} %get-tuple-element.3607), channel_id=1, source_target_pairs={{1,0},{2,1},{3,2},{4,3},{5,4},{6,5},{7,6},{8,7},{9,8},{10,9},{11,1... | collective-permute-start | bytes 73736 | tf_op jit(solution)/shard_map/while/body/eval_jaxpr/ppermute | solution.py:18
  799.4 91.8 %collective-permute-start.3 = (bf16[1,24,512]{2,1,0:T(8,128)(2,1)S(1)}, bf16[1,24,512]{2,1,0:T(8,128)(2,1)S(1)}, u32[]{:S(2)}, u32[]{:S(2)}) collective-permute-start(bf16[1,24,512]{2,1,0:T(8,128)(2,1)S(1)} %get-tuple-element.3608), channel_id=1, source_target_pairs={{0,1},{1,2},{2,3},{3,4},{4,5},{5,6},{6,7},{7,8},{8,9},{9,10},{10,1... | collective-permute-start | bytes 73736 | tf_op jit(solution)/shard_map/while/body/eval_jaxpr/ppermute | solution.py:15
  1155.7 99.6 %collective-permute-start.2 = (bf16[1,24,512]{2,1,0:T(8,128)(2,1)S(1)}, bf16[1,24,512]{2,1,0:T(8,128)(2,1)S(1)}, u32[]{:S(2)}, u32[]{:S(2)}) collective-permute-start(bf16[1,24,512]{2,1,0:T(8,128)(2,1)S(1)} %get-tuple-element.3607), channel_id=1, source_target_pairs={{1,0},{2,1},{3,2},{4,3},{5,4},{6,5},{7,6},{8,7},{9,8},{10,9},{11,1... | collective-permute-start | bytes 73736 | tf_op jit(solution)/shard_map/while/body/eval_jaxpr/ppermute | solution.py:18
  1163.2 91.7 %collective-permute-start.3 = (bf16[1,24,512]{2,1,0:T(8,128)(2,1)S(1)}, bf16[1,24,512]{2,1,0:T(8,128)(2,1)S(1)}, u32[]{:S(2)}, u32[]{:S(2)}) collective-permute-start(bf16[1,24,512]{2,1,0:T(8,128)(2,1)S(1)} %get-tuple-element.3608), channel_id=1, source_target_pairs={{0,1},{1,2},{2,3},{3,4},{4,5},{5,6},{6,7},{7,8},{8,9},{9,10},{10,1... | collective-permute-start | bytes 73736 | tf_op jit(solution)/shard_map/while/body/eval_jaxpr/ppermute | solution.py:15
  1519.5 99.6 %collective-permute-start.2 = (bf16[1,24,512]{2,1,0:T(8,128)(2,1)S(1)}, bf16[1,24,512]{2,1,0:T(8,128)(2,1)S(1)}, u32[]{:S(2)}, u32[]{:S(2)}) collective-permute-start(bf16[1,24,512]{2,1,0:T(8,128)(2,1)S(1)} %get-tuple-element.3607), channel_id=1, source_target_pairs={{1,0},{2,1},{3,2},{4,3},{5,4},{6,5},{7,6},{8,7},{9,8},{10,9},{11,1... | collective-permute-start | bytes 73736 | tf_op jit(solution)/shard_map/while/body/eval_jaxpr/ppermute | solution.py:18
  1527.0 91.7 %collective-permute-start.3 = (bf16[1,24,512]{2,1,0:T(8,128)(2,1)S(1)}, bf16[1,24,512]{2,1,0:T(8,128)(2,1)S(1)}, u32[]{:S(2)}, u32[]{:S(2)}) collective-permute-start(bf16[1,24,512]{2,1,0:T(8,128)(2,1)S(1)} %get-tuple-element.3608), channel_id=1, source_target_pairs={{0,1},{1,2},{2,3},{3,4},{4,5},{5,6},{6,7},{7,8},{8,9},{9,10},{10,1... | collective-permute-start | bytes 73736 | tf_op jit(solution)/shard_map/while/body/eval_jaxpr/ppermute | solution.py:15
  1909.8 63.7 collective-permute-start.11
  1911.7 74.0 %collective-permute-start.12 = (bf16[1,24,512]{2,1,0:T(8,128)(2,1)S(1)}, bf16[1,24,512]{2,1,0:T(8,128)(2,1)S(1)}, u32[]{:S(2)}, u32[]{:S(2)}) collective-permute-start(bf16[1,24,512]{2,1,0:T(8,128)(2,1)S(1)} %get-tuple-element.3796), channel_id=1, source_target_pairs={{1,0},{2,1},{3,2},{4,3},{5,4},{6,5},{7,6},{8,7},{9,8},{10,9},{11,1... | collective-permute-start | bytes 73736 | tf_op jit(solution)/shard_map/while/body/eval_jaxpr/ppermute | solution.py:18
  1919.1 66.7 %collective-permute-start.13 = (bf16[1,24,512]{2,1,0:T(8,128)(2,1)}, bf16[1,24,512]{2,1,0:T(8,128)(2,1)S(1)}, u32[]{:S(2)}, u32[]{:S(2)}) collective-permute-start(bf16[1,24,512]{2,1,0:T(8,128)(2,1)} %get-tuple-element.3800), channel_id=1, source_target_pairs={{1,0},{2,1},{3,2},{4,3},{5,4},{6,5},{7,6},{8,7},{9,8},{10,9},{11,1... | collective-permute-start | bytes 73736 | tf_op jit(solution)/shard_map/while/body/eval_jaxpr/ppermute | solution.py:18
  1922.9 62.9 collective-permute-start.14
  2173.1 151.0 %collective-permute-start.17 = (bf16[1,24,512]{2,1,0:T(8,128)(2,1)S(1)}, bf16[1,24,512]{2,1,0:T(8,128)(2,1)S(1)}, u32[]{:S(2)}, u32[]{:S(2)}) collective-permute-start(bf16[1,24,512]{2,1,0:T(8,128)(2,1)S(1)} %get-tuple-element.3867), channel_id=1, source_target_pairs={{0,1},{1,2},{2,3},{3,4},{4,5},{5,6},{6,7},{7,8},{8,9},{9,10},{10,1... | collective-permute-start | bytes 73736 | tf_op jit(solution)/shard_map/while/body/eval_jaxpr/ppermute | solution.py:15
  2175.1 149.1 %collective-permute-start.18 = (bf16[1,24,512]{2,1,0:T(8,128)(2,1)S(1)}, bf16[1,24,512]{2,1,0:T(8,128)(2,1)S(1)}, u32[]{:S(2)}, u32[]{:S(2)}) collective-permute-start(bf16[1,24,512]{2,1,0:T(8,128)(2,1)S(1)} %get-tuple-element.3868), channel_id=1, source_target_pairs={{1,0},{2,1},{3,2},{4,3},{5,4},{6,5},{7,6},{8,7},{9,8},{10,9},{11,1... | collective-permute-start | bytes 73736 | tf_op jit(solution)/shard_map/while/body/eval_jaxpr/ppermute | solution.py:18
  2365.1 89.8 %collective-permute-start.19 = (bf16[1,24,512]{2,1,0:T(8,128)(2,1)S(1)}, bf16[1,24,512]{2,1,0:T(8,128)(2,1)S(1)}, u32[]{:S(2)}, u32[]{:S(2)}) collective-permute-start(bf16[1,24,512]{2,1,0:T(8,128)(2,1)S(1)} %get-tuple-element.3877), channel_id=1, source_target_pairs={{0,1},{1,2},{2,3},{3,4},{4,5},{5,6},{6,7},{7,8},{8,9},{9,10},{10,1... | collective-permute-start | bytes 73736 | tf_op jit(solution)/shard_map/while/body/eval_jaxpr/ppermute | solution.py:15
  2367.1 87.9 %collective-permute-start.20 = (bf16[1,24,512]{2,1,0:T(8,128)(2,1)S(1)}, bf16[1,24,512]{2,1,0:T(8,128)(2,1)S(1)}, u32[]{:S(2)}, u32[]{:S(2)}) collective-permute-start(bf16[1,24,512]{2,1,0:T(8,128)(2,1)S(1)} %get-tuple-element.3878), channel_id=1, source_target_pairs={{1,0},{2,1},{3,2},{4,3},{5,4},{6,5},{7,6},{8,7},{9,8},{10,9},{11,1... | collective-permute-start | bytes 73736 | tf_op jit(solution)/shard_map/while/body/eval_jaxpr/ppermute | solution.py:18
  2546.9 63.6 collective-permute-start.11
  2548.8 73.9 %collective-permute-start.12 = (bf16[1,24,512]{2,1,0:T(8,128)(2,1)S(1)}, bf16[1,24,512]{2,1,0:T(8,128)(2,1)S(1)}, u32[]{:S(2)}, u32[]{:S(2)}) collective-permute-start(bf16[1,24,512]{2,1,0:T(8,128)(2,1)S(1)} %get-tuple-element.3796), channel_id=1, source_target_pairs={{1,0},{2,1},{3,2},{4,3},{5,4},{6,5},{7,6},{8,7},{9,8},{10,9},{11,1... | collective-permute-start | bytes 73736 | tf_op jit(solution)/shard_map/while/body/eval_jaxpr/ppermute | solution.py:18
  2556.2 66.6 %collective-permute-start.13 = (bf16[1,24,512]{2,1,0:T(8,128)(2,1)}, bf16[1,24,512]{2,1,0:T(8,128)(2,1)S(1)}, u32[]{:S(2)}, u32[]{:S(2)}) collective-permute-start(bf16[1,24,512]{2,1,0:T(8,128)(2,1)} %get-tuple-element.3800), channel_id=1, source_target_pairs={{1,0},{2,1},{3,2},{4,3},{5,4},{6,5},{7,6},{8,7},{9,8},{10,9},{11,1... | collective-permute-start | bytes 73736 | tf_op jit(solution)/shard_map/while/body/eval_jaxpr/ppermute | solution.py:18
  2559.9 62.9 collective-permute-start.14
  2810.2 151.6 %collective-permute-start.17 = (bf16[1,24,512]{2,1,0:T(8,128)(2,1)S(1)}, bf16[1,24,512]{2,1,0:T(8,128)(2,1)S(1)}, u32[]{:S(2)}, u32[]{:S(2)}) collective-permute-start(bf16[1,24,512]{2,1,0:T(8,128)(2,1)S(1)} %get-tuple-element.3867), channel_id=1, source_target_pairs={{0,1},{1,2},{2,3},{3,4},{4,5},{5,6},{6,7},{7,8},{8,9},{9,10},{10,1... | collective-permute-start | bytes 73736 | tf_op jit(solution)/shard_map/while/body/eval_jaxpr/ppermute | solution.py:15
  2812.1 149.7 %collective-permute-start.18 = (bf16[1,24,512]{2,1,0:T(8,128)(2,1)S(1)}, bf16[1,24,512]{2,1,0:T(8,128)(2,1)S(1)}, u32[]{:S(2)}, u32[]{:S(2)}) collective-permute-start(bf16[1,24,512]{2,1,0:T(8,128)(2,1)S(1)} %get-tuple-element.3868), channel_id=1, source_target_pairs={{1,0},{2,1},{3,2},{4,3},{5,4},{6,5},{7,6},{8,7},{9,8},{10,9},{11,1... | collective-permute-start | bytes 73736 | tf_op jit(solution)/shard_map/while/body/eval_jaxpr/ppermute | solution.py:18
  3002.8 90.2 %collective-permute-start.19 = (bf16[1,24,512]{2,1,0:T(8,128)(2,1)S(1)}, bf16[1,24,512]{2,1,0:T(8,128)(2,1)S(1)}, u32[]{:S(2)}, u32[]{:S(2)}) collective-permute-start(bf16[1,24,512]{2,1,0:T(8,128)(2,1)S(1)} %get-tuple-element.3877), channel_id=1, source_target_pairs={{0,1},{1,2},{2,3},{3,4},{4,5},{5,6},{6,7},{7,8},{8,9},{9,10},{10,1... | collective-permute-start | bytes 73736 | tf_op jit(solution)/shard_map/while/body/eval_jaxpr/ppermute | solution.py:15
  3004.8 88.2 %collective-permute-start.20 = (bf16[1,24,512]{2,1,0:T(8,128)(2,1)S(1)}, bf16[1,24,512]{2,1,0:T(8,128)(2,1)S(1)}, u32[]{:S(2)}, u32[]{:S(2)}) collective-permute-start(bf16[1,24,512]{2,1,0:T(8,128)(2,1)S(1)} %get-tuple-element.3878), channel_id=1, source_target_pairs={{1,0},{2,1},{3,2},{4,3},{5,4},{6,5},{7,6},{8,7},{9,8},{10,9},{11,1... | collective-permute-start | bytes 73736 | tf_op jit(solution)/shard_map/while/body/eval_jaxpr/ppermute | solution.py:18
  3185.0 63.6 collective-permute-start.11
  3186.9 73.9 %collective-permute-start.12 = (bf16[1,24,512]{2,1,0:T(8,128)(2,1)S(1)}, bf16[1,24,512]{2,1,0:T(8,128)(2,1)S(1)}, u32[]{:S(2)}, u32[]{:S(2)}) collective-permute-start(bf16[1,24,512]{2,1,0:T(8,128)(2,1)S(1)} %get-tuple-element.3796), channel_id=1, source_target_pairs={{1,0},{2,1},{3,2},{4,3},{5,4},{6,5},{7,6},{8,7},{9,8},{10,9},{11,1... | collective-permute-start | bytes 73736 | tf_op jit(solution)/shard_map/while/body/eval_jaxpr/ppermute | solution.py:18
  3194.3 66.6 %collective-permute-start.13 = (bf16[1,24,512]{2,1,0:T(8,128)(2,1)}, bf16[1,24,512]{2,1,0:T(8,128)(2,1)S(1)}, u32[]{:S(2)}, u32[]{:S(2)}) collective-permute-start(bf16[1,24,512]{2,1,0:T(8,128)(2,1)} %get-tuple-element.3800), channel_id=1, source_target_pairs={{1,0},{2,1},{3,2},{4,3},{5,4},{6,5},{7,6},{8,7},{9,8},{10,9},{11,1... | collective-permute-start | bytes 73736 | tf_op jit(solution)/shard_map/while/body/eval_jaxpr/ppermute | solution.py:18
  3448.2 151.6 %collective-permute-start.17 = (bf16[1,24,512]{2,1,0:T(8,128)(2,1)S(1)}, bf16[1,24,512]{2,1,0:T(8,128)(2,1)S(1)}, u32[]{:S(2)}, u32[]{:S(2)}) collective-permute-start(bf16[1,24,512]{2,1,0:T(8,128)(2,1)S(1)} %get-tuple-element.3867), channel_id=1, source_target_pairs={{0,1},{1,2},{2,3},{3,4},{4,5},{5,6},{6,7},{7,8},{8,9},{9,10},{10,1... | collective-permute-start | bytes 73736 | tf_op jit(solution)/shard_map/while/body/eval_jaxpr/ppermute | solution.py:15
  3450.1 149.7 %collective-permute-start.18 = (bf16[1,24,512]{2,1,0:T(8,128)(2,1)S(1)}, bf16[1,24,512]{2,1,0:T(8,128)(2,1)S(1)}, u32[]{:S(2)}, u32[]{:S(2)}) collective-permute-start(bf16[1,24,512]{2,1,0:T(8,128)(2,1)S(1)} %get-tuple-element.3868), channel_id=1, source_target_pairs={{1,0},{2,1},{3,2},{4,3},{5,4},{6,5},{7,6},{8,7},{9,8},{10,9},{11,1... | collective-permute-start | bytes 73736 | tf_op jit(solution)/shard_map/while/body/eval_jaxpr/ppermute | solution.py:18
  3640.9 90.2 %collective-permute-start.19 = (bf16[1,24,512]{2,1,0:T(8,128)(2,1)S(1)}, bf16[1,24,512]{2,1,0:T(8,128)(2,1)S(1)}, u32[]{:S(2)}, u32[]{:S(2)}) collective-permute-start(bf16[1,24,512]{2,1,0:T(8,128)(2,1)S(1)} %get-tuple-element.3877), channel_id=1, source_target_pairs={{0,1},{1,2},{2,3},{3,4},{4,5},{5,6},{6,7},{7,8},{8,9},{9,10},{10,1... | collective-permute-start | bytes 73736 | tf_op jit(solution)/shard_map/while/body/eval_jaxpr/ppermute | solution.py:15
  3642.8 88.2 %collective-permute-start.20 = (bf16[1,24,512]{2,1,0:T(8,128)(2,1)S(1)}, bf16[1,24,512]{2,1,0:T(8,128)(2,1)S(1)}, u32[]{:S(2)}, u32[]{:S(2)}) collective-permute-start(bf16[1,24,512]{2,1,0:T(8,128)(2,1)S(1)} %get-tuple-element.3878), channel_id=1, source_target_pairs={{1,0},{2,1},{3,2},{4,3},{5,4},{6,5},{7,6},{8,7},{9,8},{10,9},{11,1... | collective-permute-start | bytes 73736 | tf_op jit(solution)/shard_map/while/body/eval_jaxpr/ppermute | solution.py:18
  3823.0 63.6 collective-permute-start.11
  3824.9 73.9 %collective-permute-start.12 = (bf16[1,24,512]{2,1,0:T(8,128)(2,1)S(1)}, bf16[1,24,512]{2,1,0:T(8,128)(2,1)S(1)}, u32[]{:S(2)}, u32[]{:S(2)}) collective-permute-start(bf16[1,24,512]{2,1,0:T(8,128)(2,1)S(1)} %get-tuple-element.3796), channel_id=1, source_target_pairs={{1,0},{2,1},{3,2},{4,3},{5,4},{6,5},{7,6},{8,7},{9,8},{10,9},{11,1... | collective-permute-start | bytes 73736 | tf_op jit(solution)/shard_map/while/body/eval_jaxpr/ppermute | solution.py:18
  3832.3 66.6 %collective-permute-start.13 = (bf16[1,24,512]{2,1,0:T(8,128)(2,1)}, bf16[1,24,512]{2,1,0:T(8,128)(2,1)S(1)}, u32[]{:S(2)}, u32[]{:S(2)}) collective-permute-start(bf16[1,24,512]{2,1,0:T(8,128)(2,1)} %get-tuple-element.3800), channel_id=1, source_target_pairs={{1,0},{2,1},{3,2},{4,3},{5,4},{6,5},{7,6},{8,7},{9,8},{10,9},{11,1... | collective-permute-start | bytes 73736 | tf_op jit(solution)/shard_map/while/body/eval_jaxpr/ppermute | solution.py:18
  4086.3 151.6 %collective-permute-start.17 = (bf16[1,24,512]{2,1,0:T(8,128)(2,1)S(1)}, bf16[1,24,512]{2,1,0:T(8,128)(2,1)S(1)}, u32[]{:S(2)}, u32[]{:S(2)}) collective-permute-start(bf16[1,24,512]{2,1,0:T(8,128)(2,1)S(1)} %get-tuple-element.3867), channel_id=1, source_target_pairs={{0,1},{1,2},{2,3},{3,4},{4,5},{5,6},{6,7},{7,8},{8,9},{9,10},{10,1... | collective-permute-start | bytes 73736 | tf_op jit(solution)/shard_map/while/body/eval_jaxpr/ppermute | solution.py:15
  4088.2 149.7 %collective-permute-start.18 = (bf16[1,24,512]{2,1,0:T(8,128)(2,1)S(1)}, bf16[1,24,512]{2,1,0:T(8,128)(2,1)S(1)}, u32[]{:S(2)}, u32[]{:S(2)}) collective-permute-start(bf16[1,24,512]{2,1,0:T(8,128)(2,1)S(1)} %get-tuple-element.3868), channel_id=1, source_target_pairs={{1,0},{2,1},{3,2},{4,3},{5,4},{6,5},{7,6},{8,7},{9,8},{10,9},{11,1... | collective-permute-start | bytes 73736 | tf_op jit(solution)/shard_map/while/body/eval_jaxpr/ppermute | solution.py:18
  4278.9 90.2 %collective-permute-start.19 = (bf16[1,24,512]{2,1,0:T(8,128)(2,1)S(1)}, bf16[1,24,512]{2,1,0:T(8,128)(2,1)S(1)}, u32[]{:S(2)}, u32[]{:S(2)}) collective-permute-start(bf16[1,24,512]{2,1,0:T(8,128)(2,1)S(1)} %get-tuple-element.3877), channel_id=1, source_target_pairs={{0,1},{1,2},{2,3},{3,4},{4,5},{5,6},{6,7},{7,8},{8,9},{9,10},{10,1... | collective-permute-start | bytes 73736 | tf_op jit(solution)/shard_map/while/body/eval_jaxpr/ppermute | solution.py:15
  4280.9 88.2 %collective-permute-start.20 = (bf16[1,24,512]{2,1,0:T(8,128)(2,1)S(1)}, bf16[1,24,512]{2,1,0:T(8,128)(2,1)S(1)}, u32[]{:S(2)}, u32[]{:S(2)}) collective-permute-start(bf16[1,24,512]{2,1,0:T(8,128)(2,1)S(1)} %get-tuple-element.3878), channel_id=1, source_target_pairs={{1,0},{2,1},{3,2},{4,3},{5,4},{6,5},{7,6},{8,7},{9,8},{10,9},{11,1... | collective-permute-start | bytes 73736 | tf_op jit(solution)/shard_map/while/body/eval_jaxpr/ppermute | solution.py:18
  4461.1 63.5 collective-permute-start.11
  4463.0 73.9 %collective-permute-start.12 = (bf16[1,24,512]{2,1,0:T(8,128)(2,1)S(1)}, bf16[1,24,512]{2,1,0:T(8,128)(2,1)S(1)}, u32[]{:S(2)}, u32[]{:S(2)}) collective-permute-start(bf16[1,24,512]{2,1,0:T(8,128)(2,1)S(1)} %get-tuple-element.3796), channel_id=1, source_target_pairs={{1,0},{2,1},{3,2},{4,3},{5,4},{6,5},{7,6},{8,7},{9,8},{10,9},{11,1... | collective-permute-start | bytes 73736 | tf_op jit(solution)/shard_map/while/body/eval_jaxpr/ppermute | solution.py:18
  4470.4 66.5 %collective-permute-start.13 = (bf16[1,24,512]{2,1,0:T(8,128)(2,1)}, bf16[1,24,512]{2,1,0:T(8,128)(2,1)S(1)}, u32[]{:S(2)}, u32[]{:S(2)}) collective-permute-start(bf16[1,24,512]{2,1,0:T(8,128)(2,1)} %get-tuple-element.3800), channel_id=1, source_target_pairs={{1,0},{2,1},{3,2},{4,3},{5,4},{6,5},{7,6},{8,7},{9,8},{10,9},{11,1... | collective-permute-start | bytes 73736 | tf_op jit(solution)/shard_map/while/body/eval_jaxpr/ppermute | solution.py:18
  4724.3 151.6 %collective-permute-start.17 = (bf16[1,24,512]{2,1,0:T(8,128)(2,1)S(1)}, bf16[1,24,512]{2,1,0:T(8,128)(2,1)S(1)}, u32[]{:S(2)}, u32[]{:S(2)}) collective-permute-start(bf16[1,24,512]{2,1,0:T(8,128)(2,1)S(1)} %get-tuple-element.3867), channel_id=1, source_target_pairs={{0,1},{1,2},{2,3},{3,4},{4,5},{5,6},{6,7},{7,8},{8,9},{9,10},{10,1... | collective-permute-start | bytes 73736 | tf_op jit(solution)/shard_map/while/body/eval_jaxpr/ppermute | solution.py:15
  4726.2 149.7 %collective-permute-start.18 = (bf16[1,24,512]{2,1,0:T(8,128)(2,1)S(1)}, bf16[1,24,512]{2,1,0:T(8,128)(2,1)S(1)}, u32[]{:S(2)}, u32[]{:S(2)}) collective-permute-start(bf16[1,24,512]{2,1,0:T(8,128)(2,1)S(1)} %get-tuple-element.3868), channel_id=1, source_target_pairs={{1,0},{2,1},{3,2},{4,3},{5,4},{6,5},{7,6},{8,7},{9,8},{10,9},{11,1... | collective-permute-start | bytes 73736 | tf_op jit(solution)/shard_map/while/body/eval_jaxpr/ppermute | solution.py:18
  4917.0 90.2 %collective-permute-start.19 = (bf16[1,24,512]{2,1,0:T(8,128)(2,1)S(1)}, bf16[1,24,512]{2,1,0:T(8,128)(2,1)S(1)}, u32[]{:S(2)}, u32[]{:S(2)}) collective-permute-start(bf16[1,24,512]{2,1,0:T(8,128)(2,1)S(1)} %get-tuple-element.3877), channel_id=1, source_target_pairs={{0,1},{1,2},{2,3},{3,4},{4,5},{5,6},{6,7},{7,8},{8,9},{9,10},{10,1... | collective-permute-start | bytes 73736 | tf_op jit(solution)/shard_map/while/body/eval_jaxpr/ppermute | solution.py:15
  4918.9 88.2 %collective-permute-start.20 = (bf16[1,24,512]{2,1,0:T(8,128)(2,1)S(1)}, bf16[1,24,512]{2,1,0:T(8,128)(2,1)S(1)}, u32[]{:S(2)}, u32[]{:S(2)}) collective-permute-start(bf16[1,24,512]{2,1,0:T(8,128)(2,1)S(1)} %get-tuple-element.3878), channel_id=1, source_target_pairs={{1,0},{2,1},{3,2},{4,3},{5,4},{6,5},{7,6},{8,7},{9,8},{10,9},{11,1... | collective-permute-start | bytes 73736 | tf_op jit(solution)/shard_map/while/body/eval_jaxpr/ppermute | solution.py:18
  (746 other events, 16255.1 us)
Sparse Core Ops, SparseCore 0:
  5126.4 1440.4 all-reduce.71
where the time goes:
time: 6640 us; the launch traced here: 6610 us
  blocking collectives  2470 us (37%)
  waiting for transfers between devices  1450 us (22%)
  local copies, waits for them, and re-layouts  1280 us (19%)
  other arithmetic  638 us (10%)
  starting transfers between devices  371 us (6%)
  matrix products  355 us (5%)
    unnamed x2, waiting for transfers between devices  1440 us
    psum x20, blocking collectives, batch_moments(): totals = lax.psum(totals, 'rows')  1240 us
    psum x20, blocking collectives, norm_back(): totals = lax.psum(totals, 'rows')  1230 us
    while x1915, local copies, waits for them, and re-layouts  722 us
    add x20, other arithmetic, backward_step(): total_part + member  371 us
    ppermute x50, starting transfers between devices, padded_2(): lax.ppermute(lax.slice_in_dim(block, 0, width, axis=dim), axis, backward)  253 us
    dynamic_update_slice x165, local copies, waits for them, and re-layouts, per_device(): ignored, memory = lax.scan(forward_step, start_pooled, step_numbers)  192 us
  transfers between devices with their start and end apart: 111, of which 16 were waited for; matrix products, arithmetic and copies ran while one was open for 25% of the time, Pallas kernels for 0%

commit v1 on v0

v1 whole, which is shorter than its diff:
```python
import functools

import jax
import jax.numpy as jnp
import numpy as np
from jax import lax
from jax.experimental import pallas as pl
from jax.experimental.pallas import tpu as pltpu
from jax.sharding import PartitionSpec as P

MESH = pl.DeviceIdType.MESH
half = jnp.bfloat16
f32 = jnp.float32
epsilon = 1e-05
TEAM = 4

ANY = pl.BlockSpec(memory_space=pl.ANY)
VMEM = pl.BlockSpec(memory_space=pltpu.VMEM)


def sigmoid(x):
    return 0.5 * jnp.tanh(0.5 * x) + 0.5


def dot(a, b):
    return jnp.dot(a, b, preferred_element_type=f32)


def dot_nt(a, b):
    return lax.dot_general(a, b, (((1,), (1,)), ((), ())), preferred_element_type=f32)


def dot_tn(a, b):
    return lax.dot_general(a, b, (((0,), (0,)), ((), ())), preferred_element_type=f32)


class Remote:
    def __init__(self, src, dst, send, recv, to):
        self.src, self.dst, self.send, self.recv, self.to = src, dst, send, recv, to
        self.local = to == lax.axis_index("rows")

    def remote(self):
        return pltpu.make_async_remote_copy(
            src_ref=self.src,
            dst_ref=self.dst,
            send_sem=self.send,
            recv_sem=self.recv,
            device_id=(lax.axis_index("pipe"), self.to),
            device_id_type=MESH,
        )

    def start(self):
        @pl.when(self.local)
        def _():
            pltpu.make_async_copy(self.src, self.dst, self.recv).start()

        @pl.when(jnp.logical_not(self.local))
        def _():
            self.remote().start()

    def sent(self):
        @pl.when(jnp.logical_not(self.local))
        def _():
            self.remote().wait_send()


def arrived(dst, sem):
    pltpu.make_async_copy(dst, dst, sem).wait()


EDGES = 13


def section_kernel(cfg, *refs):
    M, G, H, W, C, T = cfg["M"], cfg["G"], cfg["H"], cfg["W"], cfg["C"], cfg["T"]
    R = M * G
    pix = H * W
    part = pix // M
    count = float(pix * G)
    norms = 2 + 3 * T
    (sec, sel, msk, perm, perm_t, spread, spread_edge, pool, gain, bias, wc, wi, wm, wt) = refs[:14]
    (out, bng, xu, xh, xp, xt, xv, xd5, xd5e, xd4, xd3, xd1, xd1e) = refs[14:27]
    (
        kc, ki, km, kt, rin, field, selin, chosen, uh, selh, uedge, px, ps, rb, ys, esend, erecv, ssend, srecv,
        h1, h2, h2e, t1, pr, res, dz, dh, dy5, dy5e, dy2, dy2e, dy4, dy3, dy1, dy1e, bn, bnr,
        w_sem, in_s, in_r, ed_s, ed_r, st_s, st_r, pp_s, pp_r, out_s, out_r, bn_s, bn_r, x_s, x_r,
    ) = refs[27:]
    p = lax.axis_index("pipe")
    r = lax.axis_index("rows")
    b, m = r // M, r % M
    e, e0 = m, r - m
    first, last = b == 0, b == G - 1
    CW = C * (1 + T)

    loads = {}

    def load(name, src, dst, i):
        loads[name] = pltpu.make_async_copy(src, dst, w_sem.at[i])
        loads[name].start()

    load("c0", wc.at[0], kc.at[0], 0)
    load("i", wi, ki, 1)
    load("c1", wc.at[1], kc.at[1], 2)
    load("m", wm, km, 3)
    for t in range(T):
        load("t%d" % t, wt.at[t], kt.at[t], 4 + t)

    zero_col = jnp.zeros((H, C), half)
    for a in range(3):
        rb[a, 0:H, :] = zero_col
        rb[a, H * (W + 1) : H * (W + 2), :] = zero_col
    px[pix // 4 :, :] = jnp.zeros((px.shape[0] - pix // 4, CW), half)

    @pl.when(first)
    def _():
        for s in range(EDGES):
            erecv[s, 0] = jnp.zeros((W, 1, C), f32)
        uh[0] = jnp.zeros((32, C), half)
        selh[0] = jnp.zeros((32, 128), half)

    @pl.when(last)
    def _():
        for s in range(EDGES):
            erecv[s, 1] = jnp.zeros((W, 1, C), f32)
        uh[1] = jnp.zeros((32, C), half)
        selh[1] = jnp.zeros((32, 128), half)

    bar = pltpu.get_barrier_semaphore()

    def hello(side, row):
        pl.semaphore_signal(bar, inc=1, device_id=(side, row), device_id_type=MESH)

    for d in range(1, M):
        hello(p, e0 + lax.rem(m + d, M))
    for d in range(1, G):
        hello(p, M * lax.rem(b + d, G) + m)
    hello(1 - p, r)
    tops = jnp.logical_and(m == M - 1, jnp.logical_not(last))
    bottoms = jnp.logical_and(m == 0, jnp.logical_not(first))

    @pl.when(jnp.logical_not(first))
    def _():
        hello(1 - p, r - M)
        hello(p, e0 - 1)

    @pl.when(jnp.logical_not(last))
    def _():
        hello(1 - p, r + M)
        hello(p, e0 + M)

    @pl.when(tops)
    def _():
        for j in range(M):
            hello(p, e0 + M + j)

    @pl.when(bottoms)
    def _():
        for j in range(M):
            hello(p, e0 - M + j)

    below_me, above_me = 1 - (b + 1) // G, (b + G - 1) // G
    top_member, bottom_member = (m + 1) // M, 1 - (m + M - 1) // M
    pl.semaphore_wait(
        bar, M + G - 1 + 2 * (below_me + above_me) + M * (top_member * below_me + bottom_member * above_me)
    )

    mine = pl.ds(pl.multiple_of(part * m, 16), part)
    field_moves, rest_moves, sel_moves, edge_moves = [], [], [], ([], [])
    for d in range(M):
        j = lax.rem(m + d, M)
        to = e0 + j
        field_moves.append(Remote(sec.at[j, :, 0:C], rin.at[mine, 0:C], in_s.at[0, d], in_r.at[0, m], to))
        sel_moves.append(Remote(sel.at[j], selin.at[mine], in_s.at[2, d], in_r.at[2, m], to))
        rest_moves.append(Remote(sec.at[j, :, C:CW], rin.at[mine, C:CW], in_s.at[1, d], in_r.at[1, m], to))
    for j in range(M):
        to = e0 + j
        edge_moves[0].append(
            Remote(sec.at[j, pl.ds(part - 32, 32), 0:C], uh.at[0], in_s.at[3, j], in_r.at[3, 0], to + M)
        )
        edge_moves[0].append(Remote(sel.at[j, pl.ds(part - 32, 32)], selh.at[0], in_s.at[4, j], in_r.at[3, 1], to + M))
        edge_moves[1].append(Remote(sec.at[j, pl.ds(0, 32), 0:C], uh.at[1], in_s.at[5, j], in_r.at[4, 0], to - M))
        edge_moves[1].append(Remote(sel.at[j, pl.ds(0, 32)], selh.at[1], in_s.at[6, j], in_r.at[4, 1], to - M))

    def start_field():
        for move in field_moves:
            move.start()
        for move in rest_moves:
            move.start()

    @pl.when(tops)
    def _():
        for move in edge_moves[0]:
            move.start()

    @pl.when(bottoms)
    def _():
        for move in edge_moves[1]:
            move.start()

    @pl.when(p == 0)
    def _():
        start_field()

    for move in sel_moves:
        move.start()

    row_of = lax.broadcasted_iota(jnp.int32, (H, C), 0)
    at_top, at_bottom = row_of == 0, row_of == H - 1

    def column(j):
        return pl.ds(pl.multiple_of(j * H, H), H)

    def over_columns(body, start=0, step=2):
        def several(c, carry):
            for u in range(step):
                carry = body(c * step + u, carry)
            return carry

        return lax.fori_loop(0, W // step, several, start)

    def build(j, value, above, below, up, down):
        here = pl.ds(pl.multiple_of(H + j * H, H), H)
        rb[1, here, :] = value.astype(half)
        rb[0, here, :] = (jnp.where(at_top, above, pltpu.roll(value, 1, 0)) * up).astype(half)
        rb[2, here, :] = (jnp.where(at_bottom, below, pltpu.roll(value, H - 1, 0)) * down).astype(half)

    def conv(kernel):
        total = None
        for tap in range(9):
            a, c = tap // 3, tap % 3
            term = dot(rb[a, H * c : H * c + pix, :], kernel[tap * C : (tap + 1) * C, :])
            total = term if total is None else total + term
        return total

    def conv_t(kernel):
        total = None
        for tap in range(9):
            a, c = tap // 3, tap % 3
            term = dot_nt(rb[a, H * c : H * c + pix, :], kernel[(8 - tap) * C : (9 - tap) * C, :])
            total = term if total is None else total + term
        return total

    def folded(total):
        return jnp.sum(total, 0, keepdims=True)

    def fold(x):
        return jnp.sum(x.reshape(H // 8, 8, C), 0)

    zero8 = jnp.zeros((8, C), f32)

    def edge_copy(slot, side):
        to = r - M if side == 0 else r + M
        return pltpu.make_async_remote_copy(
            src_ref=esend.at[slot, side],
            dst_ref=erecv.at[slot, 1 - side],
            send_sem=ed_s.at[slot, side],
            recv_sem=ed_r.at[slot, 1 - side],
            device_id=(p, to),
            device_id_type=MESH,
        )

    def send_edges(slot):
        @pl.when(jnp.logical_not(first))
        def _():
            edge_copy(slot, 0).start()

        @pl.when(jnp.logical_not(last))
        def _():
            edge_copy(slot, 1).start()

    def get_edges(slot):
        @pl.when(jnp.logical_not(first))
        def _():
            arrived(erecv.at[slot, 0], ed_r.at[slot, 0])

        @pl.when(jnp.logical_not(last))
        def _():
            arrived(erecv.at[slot, 1], ed_r.at[slot, 1])

    def finish_edges(slot):
        @pl.when(jnp.logical_not(first))
        def _():
            edge_copy(slot, 0).wait_send()

        @pl.when(jnp.logical_not(last))
        def _():
            edge_copy(slot, 1).wait_send()

    def stat_copy(slot, n, d):
        to = M * lax.rem(b + d, G) + m
        return pltpu.make_async_remote_copy(
            src_ref=ssend.at[pl.ds(slot, n)],
            dst_ref=srecv.at[b, pl.ds(slot, n)],
            send_sem=st_s.at[slot, d],
            recv_sem=st_r.at[slot, b],
            device_id=(p, to),
            device_id_type=MESH,
        )

    def send_sums(slot, n):
        srecv[b, slot : slot + n] = ssend[slot : slot + n]
        for d in range(1, G):
            stat_copy(slot, n, d).start()

    sums_sent = []

    def get_sums(slot, n):
        sums_sent.append((slot, n))
        for d in range(1, G):
            s = lax.rem(b + d, G)
            arrived(srecv.at[s, pl.ds(slot, n)], st_r.at[slot, s])

    def total(slot):
        acc = srecv[0, slot]
        for g in range(1, G):
            acc = acc + srecv[g, slot]
        return acc

    def put_sums(slot, s, q):
        ssend[slot] = jnp.concatenate([folded(s), folded(q)], 0)

    x_moves = []

    def post(index, src, dst, target):
        move = Remote(src, dst.at[e], x_s.at[index], x_r.at[index - (target if index in cfg["to_all"] else 0), e], e0 + target)
        move.start()
        x_moves.append(move)

    def moments(k, slot, edge=None):
        def body(j, carry):
            s, q = carry
            y = ys[k, column(j), :]
            if edge is not None:
                esend[edge, 0, j] = y[0:1]
                esend[edge, 1, j] = y[H - 1 : H]
            return s + fold(y), q + fold(y * y)

        s, q = over_columns(body, (zero8, zero8))
        put_sums(slot, s, q)

    norm = {}

    def norm_rows(k, slot):
        acc = total(slot)
        mean = acc[0:1] / count
        rs = lax.rsqrt(acc[1:2] / count - mean * mean + epsilon)
        scale = gain[k : k + 1, :] * rs
        norm[k] = (mean, rs, scale, bias[k : k + 1, :])

    def normed(k, y):
        mean, rs, scale, shift = norm[k]
        return (y - mean) * scale + shift

    def silu(x):
        return x * sigmoid(x)

    def silu_slope(x):
        s = sigmoid(x)
        return s * (1.0 + x * (1.0 - s))

    def pair(slot, j):
        return jnp.concatenate([erecv[slot, 0, j], erecv[slot, 1, j]], 0)

    nt = 2 + 3 * T
    F3, F4, F5 = 2, 2 + T, 2 + 2 * T

    def wait_field(kind, buffer):
        for k in range(M):
            arrived(buffer(k), in_r.at[kind, k])

    @pl.when(jnp.logical_not(first))
    def _():
        arrived(uh.at[0], in_r.at[3, 0])
        arrived(selh.at[0], in_r.at[3, 1])

    @pl.when(jnp.logical_not(last))
    def _():
        arrived(uh.at[1], in_r.at[4, 0])
        arrived(selh.at[1], in_r.at[4, 1])

    def start_of_field():
        wait_field(0, lambda k: rin.at[pl.ds(part * k, part), 0:C])
        field[p, :, 0:C] = dot(perm[...], rin[:, 0:C]).astype(half)

    def rest_of_field():
        wait_field(1, lambda k: rin.at[pl.ds(part * k, part), C:CW])
        for t in range(T):
            cols = slice((t + 1) * C, (t + 2) * C)
            field[p, :, cols] = dot(perm[...], rin[:, cols]).astype(half)

    @pl.when(p == 0)
    def _():
        start_of_field()

    wait_field(2, lambda k: selin.at[pl.ds(part * k, part)])
    chosen[...] = spread[...] * dot(perm[...], selin[...]).astype(half)

    def halo_copies():
        return (
            pltpu.make_async_remote_copy(
                src_ref=ps.at[pl.ds(pix // 4, 16), 0:C], dst_ref=px.at[pl.ds(pix // 4, 16), 0:C],
                send_sem=pp_s.at[1], recv_sem=pp_r.at[1], device_id=(1 - p, r + M), device_id_type=MESH),
            pltpu.make_async_remote_copy(
                src_ref=ps.at[pl.ds(pix // 4 + 16, 16), 0:C], dst_ref=px.at[pl.ds(pix // 4 + 16, 16), 0:C],
                send_sem=pp_s.at[2], recv_sem=pp_r.at[2], device_id=(1 - p, M * (b - 1) + m), device_id_type=MESH),
        )

    def pool_copy():
        return pltpu.make_async_remote_copy(
            src_ref=ps.at[pl.ds(0, pix // 4)], dst_ref=px.at[pl.ds(0, pix // 4)],
            send_sem=pp_s.at[0], recv_sem=pp_r.at[0], device_id=(1 - p, r), device_id_type=MESH)

    @pl.when(p == 1)
    def _():
        arrived(px.at[pl.ds(0, pix // 4)], pp_r.at[0])
        start_field()

        @pl.when(jnp.logical_not(first))
        def _():
            arrived(px.at[pl.ds(pix // 4, 16), 0:C], pp_r.at[1])

        @pl.when(jnp.logical_not(last))
        def _():
            arrived(px.at[pl.ds(pix // 4 + 16, 16), 0:C], pp_r.at[2])

        for t in range(1 + T):
            cols = slice(t * C, (t + 1) * C)
            field[0, :, cols] = dot(chosen[...], px[:, cols]).astype(half)
        edges = spread_edge[...] * jnp.concatenate([selh[0], selh[1]], 0)
        both = dot(edges, px[:, 0:C]).astype(half)
        uh[0] = both[0:32]
        uh[1] = both[32:64]

    above = uh[0].astype(f32)
    below = uh[1].astype(f32)
    for j in range(W):
        uedge[0, j] = above[32 - W + j : 33 - W + j]
        uedge[1, j] = below[j : j + 1]

    up = msk[0]
    down = msk[1]

    def body_u(j, carry):
        build(j, field[0, column(j), 0:C].astype(f32), uedge[0, j], uedge[1, j], up, down)
        return carry

    over_columns(body_u)
    loads["c0"].wait()
    ys[0] = conv(kc.at[0])
    moments(0, 0, 0)
    send_sums(0, 1)
    send_edges(0)

    @pl.when(p == 0)
    def _():
        rest_of_field()

    for q in range(TEAM):
        post(q, field.at[0, :, 0:C], xu, q)
    for t in range(T):
        post(8 + t, field.at[0, :, (t + 1) * C : (t + 2) * C], xv, t)
    get_sums(0, 1)
    get_edges(0)
    norm_rows(0, 0)

    def body_h1(j, carry):
        value = silu(normed(0, ys[0, column(j), :]))
        side = silu(normed(0, pair(0, j)))
        h1[column(j), :] = value.astype(half)
        build(j, value, side[0:1], side[1:2], up, down)
        return carry

    over_columns(body_h1)
    for q in range(TEAM):
        post(4 + q, h1, xh, q)

    loads["i"].wait()
    for t in range(T):
        k = 2 + 3 * t
        ys[k] = dot(h1[...], ki[t, 0:C, :]) + dot(field[0, :, (t + 1) * C : (t + 2) * C], ki[t, C : 2 * C, :])
        moments(k, F3 + t)
    send_sums(F3, T)
    loads["c1"].wait()
    ys[1] = conv(kc.at[1])
    moments(1, 1, 1)
    send_sums(1, 1)
    send_edges(1)

    get_sums(F3, T)
    loads["m"].wait()
    for t in range(T):
        k = 2 + 3 * t
        norm_rows(k, F3 + t)

        def body_t1(j, carry):
            t1[t, column(j), :] = silu(normed(k, ys[k, column(j), :])).astype(half)
            return carry

        over_columns(body_t1)
        post(11 + t, t1.at[t], xt, t)
        ys[k + 1] = dot(t1[t], km[t])
        moments(k + 1, F4 + t, 2 + t)
    send_sums(F4, T)
    for t in range(T):
        send_edges(2 + t)

    get_sums(1, 1)
    get_edges(1)
    norm_rows(1, 1)

    def body_h2(j, carry):
        value = silu(normed(1, ys[1, column(j), :])).astype(half)
        h2[column(j), :] = value
        res[column(j), 0:C] = value
        side = silu(normed(1, pair(1, j))).astype(half).astype(f32)
        h2e[j] = side
        return carry

    over_columns(body_h2)
    get_sums(F4, T)
    for t in range(T):
        k = 3 + 3 * t
        get_edges(2 + t)
        norm_rows(k, F4 + t)

        def body_p(j, carry):
            gate = sigmoid(normed(k, ys[k, column(j), :]))
            value = gate * h2[column(j), :].astype(f32)
            side = sigmoid(normed(k, pair(2 + t, j))) * h2e[j]
            pr[t, column(j), :] = value.astype(half)
            build(j, value, side[0:1], side[1:2], up, down)
            return carry

        over_columns(body_p)
        post(14 + t, pr.at[t], xp, t)
        loads["t%d" % t].wait()
        ys[k + 1] = conv(kt.at[t])
        moments(k + 1, F5 + t, 5 + t)
    send_sums(F5, T)
    for t in range(T):
        send_edges(5 + t)
    get_sums(F5, T)
    for t in range(T):
        k = 4 + 3 * t
        get_edges(5 + t)
        norm_rows(k, F5 + t)

        def body_q(j, carry):
            res[column(j), (t + 1) * C : (t + 2) * C] = silu(normed(k, ys[k, column(j), :])).astype(half)
            return carry

        over_columns(body_q)

    def out_moves(which):
        cols = slice(0, C) if which == 0 else slice(C, CW)
        moves = []
        for d in range(M):
            k = lax.rem(m + d, M)
            rows = pl.ds(pl.multiple_of(part * k, 16), part)
            moves.append(
                Remote(rin.at[rows, cols], out.at[m, :, cols], out_s.at[which, d], out_r.at[which, m], e0 + k)
            )
        return moves

    def send_result(which):
        for t in range(0, 1) if which == 0 else range(1, 1 + T):
            cols = slice(t * C, (t + 1) * C)
            rin[:, cols] = dot(perm_t[...], res[:, cols]).astype(half)
        for move in out_moves(which):
            move.start()

    @pl.when(p == 0)
    def _():
        for t in range(1 + T):
            cols = slice(t * C, (t + 1) * C)
            ps[:, cols] = dot(pool[...], res[:, cols]).astype(half)
        pool_copy().start()

        @pl.when(jnp.logical_not(last))
        def _():
            halo_copies()[0].start()

        @pl.when(jnp.logical_not(first))
        def _():
            halo_copies()[1].start()

        pool_copy().wait_send()

        @pl.when(jnp.logical_not(last))
        def _():
            halo_copies()[0].wait_send()

        @pl.when(jnp.logical_not(first))
        def _():
            halo_copies()[1].wait_send()

        arrived(px.at[pl.ds(0, pix // 4)], pp_r.at[0])
        for t in range(1 + T):
            cols = slice(t * C, (t + 1) * C)
            field[1, :, cols] = (dot(spread[...], px[:, cols]) * 0.25).astype(half)

    @pl.when(p == 1)
    def _():
        start_of_field()
        rest_of_field()
        send_result(0)
        send_result(1)

    B3, B4, B5 = nt + F3, nt + F4, nt + F5
    back = {}

    def back_rows(k, slot):
        acc = total(slot)
        mean, rs, scale, shift = norm[k]
        slope = -scale * rs * acc[1:2] / count
        back[k] = (scale, slope, -scale * acc[0:1] / count - slope * mean)
        bn[k : k + 1, :] = acc[1:2]
        bn[norms + k : norms + k + 1, :] = acc[0:1]

    def grad_pre(k, dzv, y):
        scale, slope, rest = back[k]
        return scale * dzv + slope * y + rest

    def hat(k, y):
        mean, rs, scale, shift = norm[k]
        return (y - mean) * rs

    for t in range(T):
        k = 4 + 3 * t

        def body_dz5(j, carry):
            s, q = carry
            y = ys[k, column(j), :]
            g = field[1, column(j), (t + 1) * C : (t + 2) * C].astype(f32)
            v = g * silu_slope(normed(k, y))
            dz[t, column(j), :] = v
            esend[8 + t, 0, j] = v[0:1]
            esend[8 + t, 1, j] = v[H - 1 : H]
            return s + fold(v), q + fold(v * hat(k, y))

        s, q = over_columns(body_dz5, (zero8, zero8))
        put_sums(B5 + t, s, q)
    send_sums(B5, T)
    for t in range(T):
        send_edges(8 + t)
    get_sums(B5, T)

    for t in range(T):
        k = 4 + 3 * t
        get_edges(8 + t)
        back_rows(k, B5 + t)

        def body_dy5(j, carry):
            v = grad_pre(k, dz[t, column(j), :], ys[k, column(j), :])
            side = grad_pre(k, pair(8 + t, j), pair(5 + t, j))
            dy5[t, column(j), :] = v.astype(half)
            dy5e[t, 0, j] = side[0:1]
            dy5e[t, 1, j] = side[1:2]
            build(j, v, side[0:1], side[1:2], up, down)
            return carry

        over_columns(body_dy5)
        post(17 + t, dy5.at[t], xd5, t)
        post(21 + t, dy5e.at[t], xd5e, t)
        ys[k] = conv_t(kt.at[t])

        def body_dz4(j, carry):
            s, q = carry
            dp = ys[k, column(j), :]
            y = ys[k - 1, column(j), :]
            gate = sigmoid(normed(k - 1, y))
            dgate = dp * h2[column(j), :].astype(f32)
            base = field[1, column(j), 0:C].astype(f32) if t == 0 else dh[column(j), :]
            dh[column(j), :] = base + dp * gate
            v = dgate * gate * (1.0 - gate)
            ys[k, column(j), :] = v
            return s + fold(v), q + fold(v * hat(k - 1, y))

        s, q = over_columns(body_dz4, (zero8, zero8))
        put_sums(B4 + t, s, q)
    send_sums(B4, T)

    def body_dz2(j, carry):
        s, q = carry
        y = ys[1, column(j), :]
        v = dh[column(j), :] * silu_slope(normed(1, y))
        dh[column(j), :] = v
        esend[11, 0, j] = v[0:1]
        esend[11, 1, j] = v[H - 1 : H]
        return s + fold(v), q + fold(v * hat(1, y))

    s, q = over_columns(body_dz2, (zero8, zero8))
    put_sums(nt + 1, s, q)
    send_sums(nt + 1, 1)
    send_edges(11)

    get_sums(B4, T)
    for t in range(T):
        k = 3 + 3 * t
        back_rows(k, B4 + t)

        def body_dy4(j, carry):
            dy4[t, column(j), :] = grad_pre(k, ys[k + 1, column(j), :], ys[k, column(j), :]).astype(half)
            return carry

        over_columns(body_dy4)
        post(25 + t, dy4.at[t], xd4, t)
        dz[t] = dot_nt(dy4[t], km[t])

        def body_dz3(j, carry):
            s, q = carry
            y = ys[k - 1, column(j), :]
            v = dz[t, column(j), :] * silu_slope(normed(k - 1, y))
            dz[t, column(j), :] = v
            return s + fold(v), q + fold(v * hat(k - 1, y))

        s, q = over_columns(body_dz3, (zero8, zero8))
        put_sums(B3 + t, s, q)
    send_sums(B3, T)

    get_sums(nt + 1, 1)
    get_edges(11)
    back_rows(1, nt + 1)

    def body_dy2(j, carry):
        v = grad_pre(1, dh[column(j), :], ys[1, column(j), :])
        side = grad_pre(1, pair(11, j), pair(1, j))
        dy2[column(j), :] = v.astype(half)
        dy2e[0, j] = side[0:1]
        dy2e[1, j] = side[1:2]
        build(j, v, side[0:1], side[1:2], up, down)
        return carry

    over_columns(body_dy2)
    post(20, dy2, xd5, TEAM - 1)
    post(24, dy2e, xd5e, TEAM - 1)
    dh[...] = conv_t(kc.at[1])

    get_sums(B3, T)
    for t in range(T):
        k = 2 + 3 * t
        back_rows(k, B3 + t)

        def body_dy3(j, carry):
            dy3[t, column(j), :] = grad_pre(k, dz[t, column(j), :], ys[k, column(j), :]).astype(half)
            return carry

        over_columns(body_dy3)
        post(28 + t, dy3.at[t], xd3, t)
        dh[...] += dot_nt(dy3[t], ki[t, 0:C, :])
        res[:, (t + 1) * C : (t + 2) * C] = dot_nt(dy3[t], ki[t, C : 2 * C, :]).astype(half)

    @pl.when(p == 0)
    def _():
        send_result(1)

    def body_dz1(j, carry):
        s, q = carry
        y = ys[0, column(j), :]
        v = dh[column(j), :] * silu_slope(normed(0, y))
        dh[column(j), :] = v
        esend[12, 0, j] = v[0:1]
        esend[12, 1, j] = v[H - 1 : H]
        return s + fold(v), q + fold(v * hat(0, y))

    s, q = over_columns(body_dz1, (zero8, zero8))
    put_sums(nt, s, q)
    send_sums(nt, 1)
    send_edges(12)
    get_sums(nt, 1)
    get_edges(12)
    back_rows(0, nt)

    def bn_moves():
        return [Remote(bn, bnr.at[m], bn_s.at[d], bn_r.at[m], e0 + lax.rem(m + d, M)) for d in range(M)]

    for move in bn_moves():
        move.start()

    quarter = C // TEAM

    def body_dy1(j, carry):
        v = grad_pre(0, dh[column(j), :], ys[0, column(j), :])
        side = grad_pre(0, pair(12, j), pair(0, j))
        low = v.astype(half)
        for o in range(TEAM):
            cols = slice(o * quarter, (o + 1) * quarter)
            dy1[o, column(j), :] = low[:, cols]
            dy1e[o, 0, j] = side[0:1, cols]
            dy1e[o, 1, j] = side[1:2, cols]
        build(j, v, side[0:1], side[1:2], up, down)
        return carry

    over_columns(body_dy1)
    for o in range(TEAM):
        post(31 + o, dy1.at[o], xd1, o)
        post(35 + o, dy1e.at[o], xd1e, o)
    res[:, 0:C] = conv_t(kc.at[0]).astype(half)

    @pl.when(p == 1)
    def _():
        for t in range(1 + T):
            cols = slice(t * C, (t + 1) * C)
            ps[0 : pix // 4, cols] = dot_tn(chosen[...], res[:, cols])[0 : pix // 4].astype(half)
        pool_copy().start()
        pool_copy().wait_send()

    @pl.when(p == 0)
    def _():
        send_result(0)

    for k in range(M):
        arrived(bnr.at[k], bn_r.at[k])
    acc = bnr[0]
    for k in range(1, M):
        acc = acc + bnr[k]
    bng[...] = acc
    for k in range(M):
        arrived(out.at[k, :, 0:C], out_r.at[0, k])
        arrived(out.at[k, :, C:CW], out_r.at[1, k])
    for move in out_moves(0) + out_moves(1) + bn_moves() + field_moves + rest_moves + sel_moves:
        move.sent()

    @pl.when(tops)
    def _():
        for move in edge_moves[0]:
            move.sent()

    @pl.when(bottoms)
    def _():
        for move in edge_moves[1]:
            move.sent()

    for s in range(EDGES):
        finish_edges(s)
    for slot, n in sums_sent:
        for d in range(1, G):
            stat_copy(slot, n, d).wait_send()
    for move in x_moves:
        move.sent()
    for j in range(TEAM):
        for index, dst in ((0, xu), (4, xh), (31, xd1), (35, xd1e)):
            arrived(dst.at[j], x_r.at[index, j])
    for t in range(T):

        @pl.when(e == t)
        def _():
            for j in range(TEAM):
                for index, dst in ((8, xv), (11, xt), (14, xp), (17, xd5), (21, xd5e), (25, xd4), (28, xd3)):
                    arrived(dst.at[j], x_r.at[index + t, j])

    @pl.when(e == TEAM - 1)
    def _():
        for j in range(TEAM):
            arrived(xd5.at[j], x_r.at[20, j])
            arrived(xd5e.at[j], x_r.at[24, j])


def tables(M, G, H, W):
    pix = H * W
    cm = np.zeros((pix, pix), np.float32)
    spread = np.zeros((pix, 128), np.float32)
    pool = np.zeros((128, pix), np.float32)
    edge = np.zeros((64, 128), np.float32)
    wide = W // 2
    own = pix // 4
    for i in range(H):
        for j in range(W):
            q = j * H + i
            cm[q, i * W + j] = 1
            w = (i // 2) * wide + j // 2
            spread[q, w] = 1
            pool[w, q] = 0.25
            if i >= H - 2:
                pool[own + j // 2, q] = 0.25
            if i < 2:
                pool[own + 16 + j // 2, q] = 0.25
    for j in range(W):
        edge[32 - W + j, own + j // 2] = 1
        edge[32 + j, own + 16 + j // 2] = 1
    return [jnp.asarray(v, half) for v in (cm, cm.T, spread, edge, pool)]


def gradient_kernel(cfg, *refs):
    M, G, H, W, C, T, n = cfg["M"], cfg["G"], cfg["H"], cfg["W"], cfg["C"], cfg["T"], cfg["n"]
    R = M * G
    pix = H * W
    q4 = C // TEAM
    (msk, xu, xh, xp, xt, xv, xd5, xd5e, xd4, xd3, xd1, xd1e) = refs[:12]
    (gm, g1, gi, gt) = refs[12:16]
    (va, vb, vc, vd, d5, d5e, rb, r1, d1, d1e, d3, pm, p1, pi_, pt, am, a1, ai, at, in_sem, s_sem, r_sem) = refs[16:]
    p = lax.axis_index("pipe")
    r = lax.axis_index("rows")
    e = r % TEAM
    z = r // TEAM
    task = e < T

    loads = {}

    def load(name, src, dst, i):
        loads[name] = pltpu.make_async_copy(src, dst, in_sem.at[i])
        loads[name].start()

    load("d5", xd5, d5, 0)
    load("d5e", xd5e, d5e, 1)
    load("h", xh, va, 2)

    @pl.when(task)
    def _():
        pltpu.make_async_copy(xp, vb, in_sem.at[3]).start()
        pltpu.make_async_copy(xv, vc, in_sem.at[4]).start()
        pltpu.make_async_copy(xt, vd, in_sem.at[5]).start()
        pltpu.make_async_copy(xd3, d3.at[0], in_sem.at[6]).start()
        pltpu.make_async_copy(xd4, d3.at[1], in_sem.at[7]).start()

    bar = pltpu.get_barrier_semaphore()

    def greet(i, _):
        pl.semaphore_signal(bar, inc=1, device_id=(p, lax.rem(r + TEAM * i, R)), device_id_type=MESH)
        return 0

    lax.fori_loop(1, n, greet, 0)
    pl.semaphore_wait(bar, n - 1)

    row_of = lax.broadcasted_iota(jnp.int32, (H, C), 0)
    row_of1 = lax.broadcasted_iota(jnp.int32, (H, q4), 0)

    def column(j):
        return pl.ds(pl.multiple_of(j * H, H), H)

    for j in range(TEAM):
        for a in range(3):
            rb[j, a, 0:H, :] = jnp.zeros((H, C), half)
            rb[j, a, H * (W + 1) : H * (W + 2), :] = jnp.zeros((H, C), half)
            r1[j, a, 0:H, :] = jnp.zeros((H, 3 * q4), half)
            r1[j, a, H * (W - 1) :, :] = jnp.zeros((H, 3 * q4), half)

    loads["d5"].wait()
    loads["d5e"].wait()
    for j in range(TEAM):

        def body(c, carry):
            for u in range(2):
                i = c * 2 + u
                here = pl.ds(pl.multiple_of(H + i * H, H), H)
                v = d5[j, column(i), :].astype(f32)
                rb[j, 1, here, :] = v.astype(half)
                rb[j, 0, here, :] = (jnp.where(row_of == 0, d5e[j, 0, i], pltpu.roll(v, 1, 0)) * msk[j, 0]).astype(half)
                rb[j, 2, here, :] = (
                    jnp.where(row_of == H - 1, d5e[j, 1, i], pltpu.roll(v, H - 1, 0)) * msk[j, 1]
                ).astype(half)
            return carry

        lax.fori_loop(0, W // 2, body, 0)
    loads["h"].wait()

    @pl.when(task)
    def _():
        pltpu.make_async_copy(xp, vb, in_sem.at[3]).wait()
        pltpu.make_async_copy(xv, vc, in_sem.at[4]).wait()
        pltpu.make_async_copy(xt, vd, in_sem.at[5]).wait()
        pltpu.make_async_copy(xd3, d3.at[0], in_sem.at[6]).wait()
        pltpu.make_async_copy(xd4, d3.at[1], in_sem.at[7]).wait()

    @pl.when(jnp.logical_not(task))
    def _():
        vb[...] = va[...]

    for tap in range(9):
        a, c = 2 - tap // 3, 2 - tap % 3
        acc = None
        for j in range(TEAM):
            term = dot_tn(vb[j], rb[j, a, H * c : H * c + pix, :])
            acc = term if acc is None else acc + term
        pm[tap * C : (tap + 1) * C, :] = acc.astype(half)

    pltpu.make_async_copy(xu, vb, in_sem.at[8]).start()
    pltpu.make_async_copy(xd1, d1, in_sem.at[9]).start()
    pltpu.make_async_copy(xd1e, d1e, in_sem.at[10]).start()

    def group(index, src, mine, rows):
        moves = []
        for d in range(1, n):
            to = lax.rem(z + d, n)
            moves.append(
                pltpu.make_async_remote_copy(
                    src_ref=src.at[pl.ds(pl.multiple_of(to * rows, 16), rows)],
                    dst_ref=mine.at[z],
                    send_sem=s_sem.at[index, d],
                    recv_sem=r_sem.at[index, z],
                    device_id=(p, TEAM * to + e),
                    device_id_type=MESH,
                )
            )
        return moves

    rows_m, rows_i, rows_t = 9 * C // n, 2 * C // n, C // n
    main = group(0, pm, am, rows_m)
    for move in main:
        move.start()

    @pl.when(task)
    def _():
        for part, value in ((0, va), (1, vc)):
            acc = None
            for j in range(TEAM):
                term = dot_tn(value[j], d3[0, j])
                acc = term if acc is None else acc + term
            pi_[part * C : (part + 1) * C, :] = acc.astype(half)
        acc = None
        for j in range(TEAM):
            term = dot_tn(vd[j], d3[1, j])
            acc = term if acc is None else acc + term
        pt[...] = acc.astype(half)
        for move in group(1, pi_, ai, rows_i) + group(2, pt, at, rows_t):
            move.start()

    pltpu.make_async_copy(xu, vb, in_sem.at[8]).wait()
    pltpu.make_async_copy(xd1, d1, in_sem.at[9]).wait()
    pltpu.make_async_copy(xd1e, d1e, in_sem.at[10]).wait()
    for j in range(TEAM):

        def body1(i, carry):
            v = d1[j, column(i), :].astype(f32)
            three = (
                (jnp.where(row_of1 == 0, d1e[j, 0, i], pltpu.roll(v, 1, 0)) * msk[j, 0][:, 0:q4]).astype(half),
                v.astype(half),
                (jnp.where(row_of1 == H - 1, d1e[j, 1, i], pltpu.roll(v, H - 1, 0)) * msk[j, 1][:, 0:q4]).astype(half),
            )
            for a in range(3):
                r1[j, a, column(i), q4 : 2 * q4] = three[a]
            return carry

        lax.fori_loop(0, W, body1, 0)
        for a in range(3):
            r1[j, a, H : W * H, 0:q4] = r1[j, a, 0 : (W - 1) * H, q4 : 2 * q4]
            r1[j, a, 0 : (W - 1) * H, 2 * q4 : 3 * q4] = r1[j, a, H : W * H, q4 : 2 * q4]
    for a in range(3):
        acc = None
        for j in range(TEAM):
            term = dot_tn(vb[j], r1[j, 2 - a])
            acc = term if acc is None else acc + term
        for c in range(3):
            p1[(3 * a + c) * C : (3 * a + c + 1) * C, :] = acc[:, (2 - c) * q4 : (3 - c) * q4].astype(half)
    one = group(3, p1, a1, rows_m)
    for move in one:
        move.start()

    def reduce(index, src, mine, rows, dst):
        for d in range(1, n):
            s = lax.rem(z + d, n)
            arrived(mine.at[s], r_sem.at[index, s])
        mine[z] = src[pl.ds(pl.multiple_of(z * rows, 16), rows), :]
        acc = mine[0].astype(f32)
        for s in range(1, n):
            acc = acc + mine[s].astype(f32)
        dst[...] = acc.astype(dst.dtype)

    reduce(0, pm, am, rows_m, gm)

    @pl.when(task)
    def _():
        reduce(1, pi_, ai, rows_i, gi)
        reduce(2, pt, at, rows_t, gt)

    @pl.when(jnp.logical_not(task))
    def _():
        gi[...] = jnp.zeros(gi.shape, gi.dtype)
        gt[...] = jnp.zeros(gt.shape, gt.dtype)

    reduce(3, p1, a1, rows_m, g1)
    for move in main + one:
        move.wait_send()

    @pl.when(task)
    def _():
        for move in group(1, pi_, ai, rows_i) + group(2, pt, at, rows_t):
            move.wait_send()


def per_device(cfg, section_in, image_start, pool_choice, conv_shared, task_in, task_mid, task_conv, bn_gain, bn_bias):
    M, G, H, W, C, T, n = cfg["M"], cfg["G"], cfg["H"], cfg["W"], cfg["C"], cfg["T"], cfg["n"]
    R = M * G
    pix = H * W
    part = pix // M
    rows_total = H * G
    norms = 2 + 3 * T
    CW = C * (1 + T)
    p = lax.axis_index("pipe")
    r = lax.axis_index("rows")
    b, m = r // M, r % M
    sec = section_in[0].reshape(M, part, CW)
    hp = pool_choice.shape[1]
    place = jnp.arange(4, dtype=jnp.int32).reshape(2, 1, 2)
    picked = pool_choice[:, :, None, :, None] == place[None, None]
    sel = jnp.broadcast_to(picked.reshape(M, part, 1), (M, part, 128)).astype(half)

    ones = jnp.ones((M, 1), jnp.int32)
    padded = jnp.concatenate([ones, image_start[:, 1:], ones], 1)
    links = 1.0 - lax.dynamic_slice_in_dim(padded, b * H, H + 1, 1).astype(f32)
    both = jnp.stack([links[:, :-1], links[:, 1:]], 1)
    team_masks = jnp.broadcast_to(both[..., None], (M, 2, H, C))
    own_masks = lax.dynamic_index_in_dim(team_masks, m, 0, keepdims=False)

    cm, cm_t, spread, edge, pool = tables(M, G, H, W)
    sds = jax.ShapeDtypeStruct
    exchange = [
        sds((TEAM, pix, C), half),
        sds((TEAM, pix, C), half),
        sds((TEAM, pix, C), half),
        sds((TEAM, pix, C), half),
        sds((TEAM, pix, C), half),
        sds((TEAM, pix, C), half),
        sds((TEAM, 2, W, 1, C), f32),
        sds((TEAM, pix, C), half),
        sds((TEAM, pix, C), half),
        sds((TEAM, pix, C // TEAM), half),
        sds((TEAM, 2, W, 1, C // TEAM), f32),
    ]
    dma = pltpu.SemaphoreType.DMA
    vm = pltpu.VMEM
    win = pix // 4 + 32
    outs = pl.pallas_call(
        functools.partial(section_kernel, cfg),
        name="sections",
        out_shape=[sds((M, part, CW), half), sds((2 * norms, C), f32)] + exchange,
        in_specs=[ANY, ANY] + [VMEM] * 8 + [ANY] * 4,
        out_specs=[ANY, VMEM] + [ANY] * len(exchange),
        scratch_shapes=[
            vm((2, 9 * C, C), half),
            vm((T, 2 * C, C), half),
            vm((T, C, C), half),
            vm((T, 9 * C, C), half),
            vm((pix, CW), half),
            vm((2, pix, CW), half),
            vm((pix, 128), half),
            vm((pix, 128), half),
            vm((2, 32, C), half),
            vm((2, 32, 128), half),
            vm((2, W, 1, C), f32),
            vm((win, CW), half),
            vm((win, CW), half),
            vm((3, pix + 2 * H, C), half),
            vm((norms, pix, C), f32),
            vm((EDGES, 2, W, 1, C), f32),
            vm((EDGES, 2, W, 1, C), f32),
            vm((2 * norms, 2, C), f32),
            vm((G, 2 * norms, 2, C), f32),
            vm((pix, C), half),
            vm((pix, C), half),
            vm((W, 2, C), f32),
            vm((T, pix, C), half),
            vm((T, pix, C), half),
            vm((pix, CW), half),
            vm((T, pix, C), f32),
            vm((pix, C), f32),
            vm((T, pix, C), half),
            vm((T, 2, W, 1, C), f32),
            vm((pix, C), half),
            vm((2, W, 1, C), f32),
            vm((T, pix, C), half),
            vm((T, pix, C), half),
            vm((TEAM, pix, C // TEAM), half),
            vm((TEAM, 2, W, 1, C // TEAM), f32),
            vm((2 * norms, C), f32),
            vm((M, 2 * norms, C), f32),
            dma((4 + T,)),
            dma((7, M)),
            dma((5, M)),
            dma((EDGES, 2)),
            dma((EDGES, 2)),
            dma((2 * norms, G)),
            dma((2 * norms, G)),
            dma((3,)),
            dma((3,)),
            dma((2, M)),
            dma((2, M)),
            dma((M,)),
            dma((M,)),
            dma((39,)),
            dma((39, TEAM)),
        ],
        compiler_params=pltpu.CompilerParams(
            collective_id=0, has_side_effects=True, vmem_limit_bytes=63 * 2**20
        ),
    )(sec, sel, own_masks, cm, cm_t, spread, edge, pool, bn_gain[0], bn_bias[0], conv_shared[0], task_in[0], task_mid[0], task_conv[0])
    result, bn_grads = outs[:2]

    rows_m, rows_i, rows_t = 9 * C // n, 2 * C // n, C // n
    q4 = C // TEAM
    grads = pl.pallas_call(
        functools.partial(gradient_kernel, cfg),
        name="kernel_gradients",
        out_shape=[sds((rows_m, C), half), sds((rows_m, q4), half), sds((rows_i, C), half), sds((rows_t, C), half)],
        in_specs=[VMEM] + [ANY] * 11,
        out_specs=[VMEM] * 4,
        scratch_shapes=[
            vm((TEAM, pix, C), half),
            vm((TEAM, pix, C), half),
            vm((TEAM, pix, C), half),
            vm((TEAM, pix, C), half),
            vm((TEAM, pix, C), half),
            vm((TEAM, 2, W, 1, C), f32),
            vm((TEAM, 3, pix + 2 * H, C), half),
            vm((TEAM, 3, pix, 3 * q4), half),
            vm((TEAM, pix, q4), half),
            vm((TEAM, 2, W, 1, q4), f32),
            vm((2, TEAM, pix, C), half),
            vm((9 * C, C), half),
            vm((9 * C, q4), half),
            vm((2 * C, C), half),
            vm((C, C), half),
            vm((n, rows_m, C), half),
            vm((n, rows_m, q4), half),
            vm((n, rows_i, C), half),
            vm((n, rows_t, C), half),
            dma((11,)),
            dma((4, n)),
            dma((4, n)),
        ],
        compiler_params=pltpu.CompilerParams(
            collective_id=1, has_side_effects=True, vmem_limit_bytes=60 * 2**20
        ),
    )(team_masks, *outs[2:])

    gm, g1, gi, gt = grads
    pieces = [
        gm.reshape(TEAM, -1),
        g1.reshape(TEAM, -1),
        gi.reshape(TEAM, -1),
        gt.reshape(TEAM, -1),
    ]
    packed = jnp.concatenate(pieces, 1)
    teams = [[TEAM * i + j for j in range(TEAM)] for i in range(R // TEAM)]
    swapped = lax.all_to_all(packed, "rows", 0, 0, axis_index_groups=teams, tiled=False).astype(f32)
    sizes = [v.shape[1] for v in pieces]
    o = [0, sizes[0], sizes[0] + sizes[1], sizes[0] + sizes[1] + sizes[2], sum(sizes)]
    mains = swapped[:, o[0] : o[1]]
    firsts = swapped[:, o[1] : o[2]].reshape(TEAM, -1, q4).transpose(1, 0, 2).reshape(-1)
    conv_grad = jnp.stack([firsts, mains[T]])
    return (
        result.reshape(1, M, part // W, W, CW),
        conv_grad[None],
        swapped[:T, o[2] : o[3]][None],
        swapped[:T, o[3] : o[4]][None],
        mains[:T][None],
        bn_grads[None, :norms],
        bn_grads[None, norms:],
    )


def solution(mesh):
    in_specs = (
        P("pipe", None, "rows", None, None),
        P(),
        P(None, "rows", None),
        P("pipe", None, None, None),
        P("pipe", None, None, None),
        P("pipe", None, None, None),
        P("pipe", None, None, None),
        P("pipe", None, None),
        P("pipe", None, None),
    )
    out_specs = (
        P("pipe", None, "rows", None, None),
        P("pipe", None, "rows"),
        P("pipe", None, "rows"),
        P("pipe", None, "rows"),
        P("pipe", None, "rows"),
        P("pipe", None, None),
        P("pipe", None, None),
    )
    bands = mesh.shape["rows"]

    def step(section_in, image_start, pool_choice, conv_shared, task_in, task_mid, task_conv, bn_gain, bn_bias):
        M = section_in.shape[1]
        G = bands // M
        cfg = dict(
            M=M,
            G=G,
            H=section_in.shape[2] // G,
            W=section_in.shape[3],
            C=conv_shared.shape[3],
            T=task_in.shape[1],
            n=bands // TEAM,
            to_all=frozenset(range(0, 8)) | frozenset(range(31, 39)),
        )
        return jax.shard_map(
            functools.partial(per_device, cfg), mesh=mesh, in_specs=in_specs, out_specs=out_specs, check_vma=False
        )(section_in, image_start, pool_choice, conv_shared, task_in, task_mid, task_conv, bn_gain, bn_bias)

    return step
```

time: 6640 us -> 476 us (0.07)
  blocking collectives: 2470 us -> 0 us
  waiting for transfers between devices: 1450 us -> 22.2 us
  local copies, waits for them, and re-layouts: 1280 us -> 29.7 us
  other arithmetic: 638 us -> 21.2 us
  Pallas kernels: 0 us -> 379 us
  starting transfers between devices: 371 us -> 13.6 us
  matrix products: 355 us -> 0 us
    psum x40 -> x0, blocking collectives: 2470 us -> none  [the longest x20 1240 us: batch_moments(): totals = lax.psum(totals, 'rows')]
    unnamed x2 -> x0, waiting for transfers between devices: 1440 us -> none
    while x1915 -> x0, local copies, waits for them, and re-layouts: 722 us -> none
    pallas_call x0 -> x2, Pallas kernels: none -> 379 us  [the longest x1 202 us: per_device(): pl.pallas_call(functools.partial(section_kernel, cfg), name='sections', o...]
    add x30 -> x0, other arithmetic: 371 us -> none  [the longest x20 371 us: backward_step(): total_part + member]
    ppermute x110 -> x0, starting transfers between devices: 371 us -> none  [the longest x50 253 us: padded_2(): lax.ppermute(lax.slice_in_dim(block, 0, width, axis=dim), axis, backward)]
    dot_general x165 -> x0, matrix products: 355 us -> none  [the longest x25 94.1 us: conv_backward(): jnp.einsum('rwbo,bco->rwc', stacked, kernel_blocks, preferred_element_typ...]
    dynamic_update_slice x165 -> x0, local copies, waits for them, and re-layouts: 192 us -> none  [per_device(): ignored, memory = lax.scan(forward_step, start_pooled, step_numbers)]
  transfers between devices with their start and end apart: 111 -> 1, of which waited for: 16 -> 1; matrix products, arithmetic and copies ran while one was open for 25% -> 0% of each run, Pallas kernels for 0% -> 0%
where the time goes in v1:
time: 476 us; the launch traced here: 467 us
  Pallas kernels  379 us (80%)
  local copies, waits for them, and re-layouts  29.7 us (6%)
  waiting for transfers between devices  22.2 us (5%)
  other arithmetic  21.2 us (4%)
  starting transfers between devices  13.6 us (3%)
    pallas_call x1, Pallas kernels, per_device(): pl.pallas_call(functools.partial(section_kernel, cfg), name='sections', o...  202 us
    pallas_call x1, Pallas kernels, per_device(): pl.pallas_call(functools.partial(gradient_kernel, cfg), name='kernel_grad...  178 us
    all_to_all x1, waiting for transfers between devices, per_device(): lax.all_to_all(packed, 'rows', 0, 0, axis_index_groups=teams, tiled=False)  22.2 us
    unnamed x21, local copies, waits for them, and re-layouts  21.6 us
    all_to_all x2, other arithmetic, per_device(): lax.all_to_all(packed, 'rows', 0, 0, axis_index_groups=teams, tiled=False)  19.1 us
    all_to_all x1, starting transfers between devices, per_device(): lax.all_to_all(packed, 'rows', 0, 0, axis_index_groups=teams, tiled=False)  13.6 us
  transfers between devices with their start and end apart: 1, of which 1 were waited for; matrix products, arithmetic and copies ran while one was open for 0% of the time, Pallas kernels for 0%

profile of v1, /device:TPU:8, one launch (start us, length us, event | category | flops | bytes accessed | tf_op | source)
XLA Modules:
  0.0 467.1 jit_solution(215821981522150113)
XLA Ops:
  0.7 0.8 slice.33
  1.4 0.1 pad_add_fusion
  1.5 0.1 convert_subtract_fusion
  1.6 0.1 slice_bitcast_fusion.5
  1.7 0.8 copy.50
  2.5 0.1 eq.28
  2.6 0.1 copy.51
  2.7 1.4 copy_bitcast_fusion.1
  4.1 0.7 broadcast_in_dim.36.refs_2_
  4.8 0.8 broadcast_in_dim.34.refs_1_
  5.6 201.6 %sections.1 = (bf16[4,96,2048]{2,1,0:T(8,128)(2,1)}, f32[22,512]{1,0:T(8,128)}, bf16[4,384,512]{2,1,0:T(8,128)(2,1)}, bf16[4,384,512]{2,1,0:T(8,128)(2,1)}, bf16...) custom-call(bf16[4,96,2048]{2,1,0:T(8,128)(2,1)} %bitcast.47, ...), custom_call_target="tpu_custom_call" | custom-call | tf_op jit(solution)/shard_map/sections/pallas_call | solution.py:1123
  207.2 0.8 broadcast_in_dim.37.refs_0_
  208.0 177.5 %kernel_gradients.1 = (bf16[1152,512]{1,0:T(8,128)(2,1)}, bf16[1152,128]{1,0:T(8,128)(2,1)}, bf16[256,512]{1,0:T(8,128)(2,1)}, bf16[128,512]{1,0:T(8,128)(2,1)}) custom-call(f32[4,2,16,512]{3,2,1,0:T(8,128)} %broadcast_in_dim.37.refs_0_, bf16[4,384,512]{2,1,0:T(8,128)(2,1)} %get-tuple-element.25.refs_1_, bf16[4,384,512]{2,1,0:T(8,128)(2,1)} %get-tuple-element.26.refs_2_, ...), custom_call_target="tpu_custom_call" | custom-call | tf_op jit(solution)/shard_map/kernel_gradients/pallas_call | solution.py:1191
  385.5 0.0 copy-start.3
  385.5 0.0 copy-start.2
  385.5 0.0 copy-start.1
  385.6 2.2 reshape.70
  387.8 0.0 copy-done.3
  387.8 0.1 reshape.73
  387.9 0.0 copy-done.2
  387.9 0.9 reshape.72
  388.8 0.0 copy-done.1
  388.8 0.1 reshape.71
  388.9 14.8 %maximum_bitcast_fusion = bf16[4,1,233472]{2,0,1:T(4,128)(2,1)S(1)} fusion(bf16[4,16384]{1,0:T(4,128)(2,1)S(1)} %reshape.73, bf16[4,32768]{1,0:T(4,128)(2,1)} %reshape.72, bf16[4,36864]{1,0:T(4,128)(2,1)S(1)} %reshape.71, bf16[4,147456]{1,0:T(4,128)(2,1)S(1)} %reshape.70), kind=kLoop, calls=%fused_computation.2 | loop fusion | flops 7471104 | bytes 3735552 | tf_op jit(solution)/shard_map/all_to_all | solution.py:1235
  403.7 0.5 broadcast.35
  404.2 4.3 reduce
  408.5 4.6 reshape.76
  413.1 0.0 copy-start.4
  413.1 13.6 %all-to-all-start = ((bf16[4,2,116736]{2,1,0:T(2,128)(2,1)}), bf16[4,2,116736]{2,1,0:T(2,128)(2,1)S(1)}, u32[]{:S(2)}, u32[]{:S(2)}) async-start(bf16[4,2,116736]{2,1,0:T(2,128)(2,1)} %reshape.76), calls=%async_computation | async-start | bytes 3735552 | tf_op jit(solution)/shard_map/all_to_all | solution.py:1235
  426.7 0.0 copy-done.4
  426.8 0.6 copy.59
  427.4 0.6 copy.58
  428.0 22.2 %all-to-all-done = bf16[4,2,116736]{2,1,0:T(2,128)(2,1)S(1)} async-done(((bf16[4,2,116736]{2,1,0:T(2,128)(2,1)}), bf16[4,2,116736]{2,1,0:T(2,128)(2,1)S(1)}, u32[]{:S(2)}, u32[]{:S(2)}) %all-to-all-start) | async-done | bytes 1867808 | tf_op jit(solution)/shard_map/all_to_all | solution.py:1235
  450.3 3.1 reshape.77
  453.4 4.4 copy.66
  457.9 0.7 slice.44
  458.6 0.2 slice_bitcast_fusion
  458.8 0.9 copy.56
  459.7 1.1 copy.55
  460.8 2.8 copy.57
  463.7 0.0 copy-start
  463.7 1.9 maximum_bitcast_fusion.1
  465.6 0.0 copy-done
  465.6 1.1 copy.69
  (12 shorter events, 0.2 us)
Async XLA Ops:
  385.5 2.3 copy-start.3
  385.5 2.4 copy-start.2
  385.5 3.2 copy-start.1
  413.1 13.6 %copy-start.4 = (f32[22,512]{1,0:T(8,128)S(1)}, f32[22,512]{1,0:T(8,128)}, u32[]{:S(2)}) copy-start(f32[22,512]{1,0:T(8,128)} %get-tuple-element.40) | copy-start | bytes 135172
  413.1 37.2 %all-to-all-start = ((bf16[4,2,116736]{2,1,0:T(2,128)(2,1)}), bf16[4,2,116736]{2,1,0:T(2,128)(2,1)S(1)}, u32[]{:S(2)}, u32[]{:S(2)}) async-start(bf16[4,2,116736]{2,1,0:T(2,128)(2,1)} %reshape.76), calls=%async_computation | async-start | bytes 3735552 | tf_op jit(solution)/shard_map/all_to_all | solution.py:1235
  463.7 1.9 copy-start
